TPU v7x, 32 devices: a whole 2x2x4 slice. The times are simulated.
32 devices in a mesh: mem: 4 (over z), reg: 8 (over y, x, core).
Axes of the slice: x: 2, y: 2, z: 4, core: 2. Of those that a mesh axis runs over, the one named last changes fastest.
Arguments:
- background: bfloat16 [240, 8, 4096], P('mem', 'reg'), may hold values from -6 to 6
- obs_index: int32 [8, 4, 512], P('reg'), may hold values from 0 to 1023
- yobs: bfloat16 [8, 4, 512], P('reg', 'mem'), may hold values from -6 to 6
- loc_list: int32 [8, 4, 2048], P('reg', 'mem'), may hold values from 0 to 4607, as said below
- loc_count: int32 [8, 4], P('reg', 'mem'), may hold values from 256 to 2048, as said below
- loc_weight: float32 [8, 4, 2048], P('reg', 'mem'), may hold values from 0.03 to 0.6
Outputs:
- analysis: bfloat16 [240, 8, 4096], P('mem', 'reg')
Inputs may be any that keep to these rules, and one draw needn't show every extreme that they name: `loc_list`: for each region the first loc_count entries name distinct candidates; later entries are candidate numbers that carry no weight. `loc_count`: some region has exactly 2048 entries and some exactly 256.
All inputs are finite; a program needn't handle non-finite values.
Results may differ from a plain program's by a relative error of at most 0.006.
Values may be sent and summed in bfloat16 or wider, within the bound.
A program may use at most 64 MiB of HBM per device.

v0:
```python
import math

import jax
import jax.numpy as jnp
from jax import lax
from jax.sharding import PartitionSpec as P

NS_STEPS = 5


inflation = 1.1


def with_halo(shard, sides, width):
    for axis, dim in sides:
        size, length = (lax.axis_size(axis), shard.shape[dim])
        up = [(i, (i + 1) % size) for i in range(size)]
        down = [(j, i) for i, j in up]
        last = lax.slice_in_dim(shard, length - width, length, axis=dim)
        initial = lax.slice_in_dim(shard, 0, width, axis=dim)
        before = lax.ppermute(last, axis, up)
        after = lax.ppermute(initial, axis, down)
        shard = jnp.concatenate([before, shard, after], axis=dim)
    return shard


def observe(states, indices):
    cell_count = states.shape[2]
    by_region = jnp.transpose(states, (1, 0, 2))

    def one_region(pair):
        region_cells, region_indices = pair
        cell_ids = lax.broadcasted_iota(jnp.int32, (cell_count, region_indices.shape[0]), 0)
        picker = (cell_ids == region_indices[None, :]).astype(jnp.bfloat16)
        return jnp.dot(region_cells, picker, preferred_element_type=jnp.float32).astype(
            jnp.bfloat16
        )

    picked = lax.map(one_region, (by_region, indices))
    return jnp.transpose(picked, (1, 0, 2))


def newton_root(gram_matrix):
    size = gram_matrix.shape[0]
    identity = jnp.eye(size, dtype=jnp.float32)
    norm_value = jnp.sqrt(jnp.sum(gram_matrix * gram_matrix))
    current = gram_matrix / norm_value
    inverse_root = identity
    for iteration in range(NS_STEPS):
        correction = 1.5 * identity - 0.5 * jnp.dot(
            inverse_root, current, precision=lax.Precision.HIGHEST
        )
        current = jnp.dot(current, correction, precision=lax.Precision.HIGHEST)
        inverse_root = jnp.dot(correction, inverse_root, precision=lax.Precision.HIGHEST)
    return (inverse_root, norm_value)


def row_products(left_rows, right_rows):
    return lax.dot_general(
        left_rows, right_rows, (((0,), (0,)), ((), ())), preferred_element_type=jnp.float32
    )


def member_mean(rows):
    members = rows.shape[0]
    ones_row = jnp.ones((members,), jnp.bfloat16)
    return jnp.dot(ones_row, rows, preferred_element_type=jnp.float32) / members


def list_products(weighted, local_rows, local_innov):
    gram_matrix = row_products(weighted, local_rows)
    drive_vector = row_products(weighted, local_innov)
    return (gram_matrix, drive_vector)


def analyze(own_state, candidates, obs_order, obs_count, obs_taper):
    members = own_state.shape[0]
    state_mean = member_mean(own_state)
    state_pert = (own_state - state_mean).astype(jnp.bfloat16)
    ensemble = candidates[:members]
    obs_mean = member_mean(ensemble)
    obs_pert = (ensemble - obs_mean).astype(jnp.bfloat16)
    innovation = (candidates[members] - obs_mean).astype(jnp.bfloat16)
    pert_rows = jnp.transpose(obs_pert)
    local_rows = jnp.take(pert_rows, obs_order, axis=0)
    local_innov = jnp.take(innovation, obs_order)
    positions = jnp.arange(obs_order.shape[0], dtype=jnp.int32)
    live_weight = jnp.where(positions < obs_count, obs_taper, jnp.float32(0.0))
    weighted = (local_rows * live_weight[:, None]).astype(jnp.bfloat16)
    gram_matrix, drive_vector = list_products(weighted, local_rows, local_innov)
    gram_matrix = gram_matrix + (members - 1) / inflation * jnp.eye(members, dtype=jnp.float32)
    inverse_root, norm_value = newton_root(gram_matrix)
    mean_shift = jnp.dot(
        inverse_root,
        jnp.dot(inverse_root, drive_vector, precision=lax.Precision.HIGHEST),
        precision=lax.Precision.HIGHEST,
    )
    weights = (
        math.sqrt(members - 1) / jnp.sqrt(norm_value) * inverse_root
        + (mean_shift / norm_value)[:, None]
    )
    weights = weights.astype(jnp.bfloat16)
    update = jnp.dot(weights.T, state_pert, preferred_element_type=jnp.float32)
    return (state_mean + update).astype(jnp.bfloat16)


def local(background, obs_index, yobs, loc_list, loc_count, loc_weight):
    region_count = yobs.shape[1]
    obs_width = yobs.shape[2]
    state = lax.all_to_all(background, "mem", split_axis=2, concat_axis=0, tiled=True)
    ensemble_size = state.shape[0]
    own_indices = lax.dynamic_slice_in_dim(
        obs_index[0], lax.axis_index("mem") * region_count, region_count, 0
    )
    observed = observe(state, own_indices)
    observed = observed.reshape(ensemble_size, 1, region_count, obs_width)
    stacked = jnp.concatenate([observed, yobs.reshape(1, 1, region_count, obs_width)], axis=0)
    extended = with_halo(stacked, (("mem", 2), ("reg", 1)), 1)
    candidates = extended.reshape(ensemble_size + 1, 9 * obs_width)
    results = [
        analyze(state[:, 0, :], candidates, loc_list[0, 0], loc_count[0, 0], loc_weight[0, 0])
    ]
    analysis = jnp.stack(results, axis=1)
    return lax.all_to_all(analysis, "mem", split_axis=0, concat_axis=2, tiled=True)


def solution(mesh):
    return jax.shard_map(
        local,
        mesh=mesh,
        in_specs=(
            P("mem", "reg", None),
            P("reg", None, None),
            P("reg", "mem", None),
            P("reg", "mem", None),
            P("reg", "mem"),
            P("reg", "mem", None),
        ),
        out_specs=P("mem", "reg", None),
        check_vma=False,
    )
```

profile of v0, /device:TPU:0, one launch (start us, length us, event | category | flops | bytes accessed | tf_op | source)
XLA Modules:
  0.0 154.5 jit_solution(10951781149504127201)
XLA Ops:
  0.0 0.0 copy-start
  0.0 4.9 %copy.19 = bf16[60,1,4096]{0,1,2:T(2,128)(2,1)S(1)} copy(bf16[60,1,4096]{2,0,1:T(8,128)(2,1)} %param.6) | data formatting | bytes 983040 | tf_op args[0]
  4.9 0.5 broadcast.86
  5.4 22.3 %reduce.5 = bf16[4096,60]{1,0:T(8,128)(2,1)S(1)} reduce(bf16[4096,1,60]{2,1,0:T(2,128)(2,1)S(1)} %bitcast.71, bf16[]{:T(256)} %broadcast.86), dimensions={1}, to_apply=%bitcast.34.reduce_sub_computation | reduce | bytes 983042
  27.7 3.6 %reshape.92 = bf16[4,2,30720]{2,1,0:T(2,128)(2,1)} reshape(bf16[4096,60]{1,0:T(8,128)(2,1)S(1)} %reduce.5) | data formatting | bytes 983040
  31.4 6.3 %all-to-all-start = ((bf16[4,2,30720]{2,1,0:T(2,128)(2,1)}), bf16[4,2,30720]{2,1,0:T(2,128)(2,1)S(1)}, u32[]{:S(2)}, u32[]{:S(2)}) async-start(bf16[4,2,30720]{2,1,0:T(2,128)(2,1)} %reshape.92), calls=%async_computation | async-start | bytes 983040 | tf_op jit(solution)/shard_map/all_to_all | solution.py:110
  37.7 0.0 copy-done
  37.7 13.8 %all-to-all-done = bf16[4,2,30720]{2,1,0:T(2,128)(2,1)S(1)} async-done(((bf16[4,2,30720]{2,1,0:T(2,128)(2,1)}), bf16[4,2,30720]{2,1,0:T(2,128)(2,1)S(1)}, u32[]{:S(2)}, u32[]{:S(2)}) %all-to-all-start) | async-done | bytes 491552 | tf_op jit(solution)/shard_map/all_to_all | solution.py:110
  51.5 3.6 %reshape.93 = bf16[4096,1,60]{2,1,0:T(2,128)(2,1)S(1)} reshape(bf16[4,2,30720]{2,1,0:T(2,128)(2,1)S(1)} %all-to-all-done) | data formatting | bytes 983040
  55.2 2.4 %copy.20 = bf16[60,1,4096]{2,0,1:T(8,128)(2,1)S(1)} copy(bf16[60,1,4096]{0,1,2:T(2,128)(2,1)S(1)} %bitcast.70) | data formatting | bytes 983040 | tf_op jit(solution)/shard_map/all_to_all | solution.py:110
  57.5 0.0 copy-start.4
  57.5 0.3 all_to_all.25
  57.8 0.0 copy-start.3
  57.8 0.2 copy.21
  58.0 0.0 copy-start.5
  58.0 0.1 squeeze.21
  58.1 0.5 fusion.7
  58.7 1.5 collective-permute-start.1
  60.2 0.6 collective-permute-start
  60.8 10.5 %collective-permute-done.1 = bf16[241,1,1,512]{3,0,2,1:T(8,128)(2,1)S(1)} collective-permute-done((bf16[241,1,1,512]{3,0,2,1:T(8,128)(2,1)S(1)}, bf16[241,1,1,512]{3,0,2,1:T(8,128)(2,1)S(1)}, u32[]{:S(2)}, u32[]{:S(2)}) %collective-permute-start.1) | collective-permute-done | bytes 246816 | tf_op jit(solution)/shard_map/ppermute | solution.py:22
  71.3 0.0 collective-permute-done
  71.3 0.1 pad_maximum_fusion.1
  71.4 0.1 collective-permute-start.3
  71.5 0.5 collective-permute-start.2
  72.6 0.2 fusion.26
  72.8 14.9 %collective-permute-done.3 = bf16[241,1,3,512]{3,0,2,1:T(8,128)(2,1)S(1)} collective-permute-done((bf16[241,1,3,512]{3,0,2,1:T(8,128)(2,1)S(1)}, bf16[241,1,3,512]{3,0,2,1:T(8,128)(2,1)S(1)}, u32[]{:S(2)}, u32[]{:S(2)}) %collective-permute-start.3) | collective-permute-done | bytes 740384 | tf_op jit(solution)/shard_map/ppermute | solution.py:22
  87.7 4.1 %collective-permute-done.2 = bf16[241,1,3,512]{3,0,2,1:T(8,128)(2,1)S(1)} collective-permute-done((bf16[241,1,3,512]{3,0,2,1:T(8,128)(2,1)S(1)}, bf16[241,1,3,512]{3,0,2,1:T(8,128)(2,1)S(1)}, u32[]{:S(2)}, u32[]{:S(2)}) %collective-permute-start.2) | collective-permute-done | bytes 740384 | tf_op jit(solution)/shard_map/ppermute | solution.py:21
  91.8 0.1 fusion.23
  91.8 0.3 pad_maximum_fusion
  92.1 1.6 %slice.17 = bf16[240,3,3,512]{3,0,2,1:T(8,128)(2,1)} slice(bf16[241,3,3,512]{3,0,2,1:T(8,128)(2,1)S(1)} %pad_maximum_fusion), slice={[0:240], [0:3], [0:3], [0:512]} | slice | bytes 4423680 | tf_op jit(solution)/shard_map/slice | solution.py:80
  93.7 2.8 %copy.22 = bf16[240,3,3,512]{0,3,2,1:T(8,128)(2,1)S(1)} copy(bf16[240,3,3,512]{3,0,2,1:T(8,128)(2,1)} %slice.17) | data formatting | bytes 4423680 | tf_op jit(solution)/shard_map/slice | solution.py:80
  96.5 0.0 copy-start.1
  96.5 1.4 copy-done.1
  97.9 0.7 convolution_reduce_fusion
  98.7 3.2 %fusion = bf16[4608,240]{1,0:T(8,128)(2,1)S(1)} fusion(f32[4608]{0:T(1024)S(1)} %get-tuple-element.20, bf16[240,3,3,512]{0,3,2,1:T(8,128)(2,1)} %copy-done.1), kind=kLoop, calls=%fused_computation.3 | loop fusion | flops 3317760 | bytes 4442112 | tf_op jit(solution)/shard_map/transpose | solution.py:84
  101.9 9.0 %gather_fusion = bf16[2048,240]{1,0:T(8,128)(2,1)} fusion(bf16[4608,240]{1,0:T(8,128)(2,1)S(1)} %fusion, s32[2048]{0:T(1024)S(1)} %broadcast_clamp_fusion), kind=kCustom, calls=%fused_computation | custom fusion | bytes 1974272 | tf_op jit(solution)/shard_map/jit(_take)/gather | solution.py:85
  110.9 13.1 %gather_fusion.1 = bf16[2048]{0:T(1024)(128)(2,1)S(1)} fusion(bf16[4608]{0:T(1024)(128)(2,1)S(1)} %get-tuple-element.18, s32[2048]{0:T(1024)S(1)} %broadcast_clamp_fusion), kind=kCustom, calls=%fused_computation.1 | custom fusion | bytes 16384 | tf_op jit(solution)/shard_map/jit(_take)/gather | solution.py:86
  124.0 2.0 %multiply_reduce_fusion = (f32[]{:T(128)}, f32[240,240]{1,0:T(8,128)S(1)}) fusion(bf16[2048,240]{1,0:T(8,128)(2,1)S(1)} %copy-done.2, pred[2048]{0:T(1024)(128)(4,1)S(1)} %get-tuple-element.16, f32[2048]{0:T(1024)S(1)} %fusion.24), kind=kOutput, calls=%fused_computation.38 | convolution fusion | flops 238675200 | bytes 1223684 | tf_op jit(solution)/shard_map/dot_general | solution.py:59
  126.7 0.3 fusion.12
  127.1 0.3 fusion.19
  127.3 0.4 fusion.22
  127.7 0.4 fusion.11
  128.1 0.4 fusion.32
  128.5 0.4 fusion.33
  128.8 0.4 fusion.10
  129.2 0.4 fusion.34
  129.6 0.4 fusion.35
  130.0 0.4 fusion.9
  130.3 0.4 fusion.36
  130.7 0.4 fusion.37
  131.1 0.4 fusion.8
  131.5 0.4 fusion.38
  131.9 0.7 fusion.14
  132.6 0.3 convolution_bitcast_fusion
  132.9 0.3 fusion.39
  133.3 0.4 fusion.5
  133.7 0.9 reduce.6
  134.6 0.3 reshape.94
  134.9 14.6 %all_to_all.33 = bf16[4,2,30720]{2,1,0:T(2,128)(2,1)S(1)} all-to-all(bf16[4,2,30720]{2,1,0:T(2,128)(2,1)S(1)} %reshape.94), channel_id=1, replica_groups=mesh['mem'=4,'reg'=8] {'mem'}, dimensions={0} | all-to-all | bytes 983040 | tf_op jit(solution)/shard_map/all_to_all | solution.py:124
  149.5 0.5 reshape.95
  150.0 2.9 %reduce.2 = bf16[240,1024]{1,0:T(8,128)(2,1)S(1)} reduce(bf16[240,1,1024]{2,1,0:T(2,128)(2,1)S(1)} %reshape.95, bf16[]{:T(256)} %constant.75), dimensions={1}, to_apply=%all_to_all.27.reduce_sub_computation | reduce | bytes 983042 | tf_op jit(solution)/shard_map/all_to_all | solution.py:124
  152.9 0.1 all_to_all.28
  153.0 0.4 copy.24
  153.4 1.1 all_to_all.30
  (16 shorter events, 0.1 us)
Async XLA Ops:
  0.0 37.7 %copy-start = (s32[1,4,512]{2,1,0:T(4,128)S(1)}, s32[1,4,512]{2,1,0:T(4,128)}, u32[]{:S(2)}) copy-start(s32[1,4,512]{2,1,0:T(4,128)} %param.7) | copy-start | bytes 24580
  31.4 20.1 %all-to-all-start = ((bf16[4,2,30720]{2,1,0:T(2,128)(2,1)}), bf16[4,2,30720]{2,1,0:T(2,128)(2,1)S(1)}, u32[]{:S(2)}, u32[]{:S(2)}) async-start(bf16[4,2,30720]{2,1,0:T(2,128)(2,1)} %reshape.92), calls=%async_computation | async-start | bytes 983040 | tf_op jit(solution)/shard_map/all_to_all | solution.py:110
  57.5 1.1 copy-start.4
  57.8 3.0 %copy-start.3 = (s32[1,1,2048]{2,1,0:T(1,128)S(1)}, s32[1,1,2048]{2,1,0:T(1,128)}, u32[]{:S(2)}) copy-start(s32[1,1,2048]{2,1,0:T(1,128)} %param.9) | copy-start | bytes 24580
  58.0 14.6 %copy-start.5 = (f32[1,1,2048]{2,1,0:T(1,128)S(1)}, f32[1,1,2048]{2,1,0:T(1,128)}, u32[]{:S(2)}) copy-start(f32[1,1,2048]{2,1,0:T(1,128)} %param.11) | copy-start | bytes 24580
  58.7 12.6 %collective-permute-start.1 = (bf16[241,1,1,512]{3,0,2,1:T(8,128)(2,1)S(1)}, bf16[241,1,1,512]{3,0,2,1:T(8,128)(2,1)S(1)}, u32[]{:S(2)}, u32[]{:S(2)}) collective-permute-start(bf16[241,1,1,512]{3,0,2,1:T(8,128)(2,1)S(1)} %pad_maximum_fusion.2), channel_id=1, source_target_pairs={{8,0},{16,8},{24,16},{0,24},{9,1},{17,9},{25,17},{1,25},{10,2},{18... | collective-permute-start | bytes 740360 | tf_op jit(solution)/shard_map/ppermute | solution.py:22
  60.2 11.1 %collective-permute-start = (bf16[241,1,1,512]{3,0,2,1:T(8,128)(2,1)S(1)}, bf16[241,1,1,512]{3,0,2,1:T(8,128)(2,1)S(1)}, u32[]{:S(2)}, u32[]{:S(2)}) collective-permute-start(bf16[241,1,1,512]{3,0,2,1:T(8,128)(2,1)S(1)} %pad_maximum_fusion.2), channel_id=1, source_target_pairs={{0,8},{8,16},{16,24},{24,0},{1,9},{9,17},{17,25},{25,1},{2,10},{10... | collective-permute-start | bytes 740360 | tf_op jit(solution)/shard_map/ppermute | solution.py:21
  71.4 16.3 %collective-permute-start.3 = (bf16[241,1,3,512]{3,0,2,1:T(8,128)(2,1)S(1)}, bf16[241,1,3,512]{3,0,2,1:T(8,128)(2,1)S(1)}, u32[]{:S(2)}, u32[]{:S(2)}) collective-permute-start(bf16[241,1,3,512]{3,0,2,1:T(8,128)(2,1)S(1)} %pad_maximum_fusion.1), channel_id=1, source_target_pairs={{1,0},{2,1},{3,2},{4,3},{5,4},{6,5},{7,6},{0,7},{9,8},{10,9},{11,1... | collective-permute-start | bytes 2221064 | tf_op jit(solution)/shard_map/ppermute | solution.py:22
  71.5 20.3 %collective-permute-start.2 = (bf16[241,1,3,512]{3,0,2,1:T(8,128)(2,1)S(1)}, bf16[241,1,3,512]{3,0,2,1:T(8,128)(2,1)S(1)}, u32[]{:S(2)}, u32[]{:S(2)}) collective-permute-start(bf16[241,1,3,512]{3,0,2,1:T(8,128)(2,1)S(1)} %pad_maximum_fusion.1), channel_id=1, source_target_pairs={{0,1},{1,2},{2,3},{3,4},{4,5},{5,6},{6,7},{7,0},{8,9},{9,10},{10,1... | collective-permute-start | bytes 2221064 | tf_op jit(solution)/shard_map/ppermute | solution.py:21
  96.5 1.4 copy-start.1
  110.9 13.1 %copy-start.2 = (bf16[2048,240]{1,0:T(8,128)(2,1)S(1)}, bf16[2048,240]{1,0:T(8,128)(2,1)}, u32[]{:S(2)}) copy-start(bf16[2048,240]{1,0:T(8,128)(2,1)} %gather_fusion) | copy-start | bytes 2949124
where the time goes:
time: 155 us
  local copies, waits for them, and re-layouts  45.9 us (30%)
  waiting for transfers between devices  43.2 us (28%)
  other arithmetic  29.8 us (19%)
  blocking collectives  14.6 us (9%)
  matrix products  10.2 us (7%)
  starting transfers between devices  8.95 us (6%)
  between operations  1.84 us (1%)
    ppermute x2, waiting for transfers between devices, with_halo(): after = lax.ppermute(initial, axis, down)  25.4 us
    unnamed x1, other arithmetic  22.3 us
    unnamed x18, local copies, waits for them, and re-layouts  14.9 us
    all_to_all x1, blocking collectives, local(): lax.all_to_all(analysis, 'mem', split_axis=0, concat_axis=2, tiled=True)  14.6 us
    all_to_all x1, waiting for transfers between devices, local(): lax.all_to_all(background, 'mem', split_axis=2, concat_axis=0, tiled=True)  13.8 us
    gather x1, local copies, waits for them, and re-layouts, analyze(): local_innov = jnp.take(innovation, obs_order)  13.1 us
    gather x1, local copies, waits for them, and re-layouts, analyze(): local_rows = jnp.take(pert_rows, obs_order, axis=0)  9 us
    all_to_all x1, starting transfers between devices, local(): lax.all_to_all(background, 'mem', split_axis=2, concat_axis=0, tiled=True)  6.32 us
  transfers between devices with their start and end apart: 5, of which 4 were waited for; matrix products, arithmetic and copies ran while one was open for 0% of the time, Pallas kernels for 0%

commit v1 on v0

v1 whole, which is shorter than its diff:
```python
import functools
import math

import jax
import jax.numpy as jnp
from jax import lax
from jax.experimental import pallas as pl
from jax.experimental.pallas import tpu as pltpu
from jax.sharding import PartitionSpec as P

NS_STEPS = 5
INFLATION = 1.1
MESH = pl.DeviceIdType.MESH
F32 = jnp.float32
BF16 = jnp.bfloat16


def split(x):
    high = x.astype(BF16)
    return high, (x - high.astype(F32)).astype(BF16)


def mm(a, b):
    return (
        jnp.dot(a[0], b[1], preferred_element_type=F32)
        + jnp.dot(a[1], b[0], preferred_element_type=F32)
        + jnp.dot(a[0], b[0], preferred_element_type=F32)
    )


def dot_t(a, b):
    return lax.dot_general(a, b, (((1,), (1,)), ((), ())), preferred_element_type=F32)


def newton(gram, norm, eye, steps):
    current = gram * (1.0 / norm)
    root = None
    for step in range(steps):
        last = step == steps - 1
        if root is None:
            corr = 1.5 * eye - 0.5 * current
            corr_s = split(corr)
            root = corr
        else:
            cur_s, root_s = split(current), split(root)
            corr = 1.5 * eye - 0.5 * mm(root_s, cur_s)
            corr_s = split(corr)
            root = mm(corr_s, root_s)
        if not last:
            current = mm(split(current), corr_s)
    return root


def kernel(
    n, regs, m, pad, width, cells,
    bg_ref, idx_ref, yobs_ref, list_ref, count_ref, weight_ref,
    out_ref,
    bgp, obs_loc, obuf, sbuf, wd, wbuf, yloc, ybuf, pert, gsend, grecv, wt, oloc,
    obs_ss, obs_rs, st_ss, st_rs, w_ss, w_rs, y_ss, y_rs, g_ss, g_rs, o_ss, o_rs,
):
    me, col = lax.axis_index("mem"), lax.axis_index("reg")
    left, right = lax.rem(col + regs - 1, regs), lax.rem(col + 1, regs)
    members, total = n * m, n * pad
    lanes = 128
    strips = width // lanes
    block = wd.shape[0] // 3

    def peer(d):
        return lax.rem(me + d, n)

    barrier = pltpu.get_barrier_semaphore()
    for d in range(1, n):
        pl.semaphore_signal(barrier, inc=1, device_id=(peer(d), col), device_id_type=MESH)
    for c in (left, right):
        pl.semaphore_signal(barrier, inc=1, device_id=(me, c), device_id_type=MESH)

    def send(src, dst, ss, rs, device):
        copy = pltpu.make_async_remote_copy(
            src_ref=src, dst_ref=dst, send_sem=ss, recv_sem=rs,
            device_id=device, device_id_type=MESH,
        )
        copy.start()
        return copy

    tail = (m // 16) * 16
    for q in range(n):
        bgp[q, tail:pad, :] = jnp.zeros((pad - tail, cells), BF16)
        bgp[q, 0:m, :] = bg_ref[:, q * cells:(q + 1) * cells]

    length = list_ref.shape[1]
    place = lax.broadcasted_iota(jnp.int32, (1, length), 1)
    live = jnp.where(place < count_ref[...], weight_ref[...], 0.0)
    part0 = live.astype(BF16)
    rest = live - part0.astype(F32)
    part1 = rest.astype(BF16)
    part2 = (rest - part1.astype(F32)).astype(BF16)
    cand = list_ref[...]
    strip = cand // lanes
    lane = cand - strip * lanes
    group = strip // (3 * strips)
    strip = strip + group * (block - 3 * strips)
    rows_at = lax.broadcasted_iota(jnp.int32, (3 * block, length), 0) == strip
    lanes_at = lax.broadcasted_iota(jnp.int32, (lanes, length), 0) == lane
    lane_hot = jnp.where(lanes_at, 1.0, 0.0).astype(BF16)
    spread = [
        dot_t(jnp.where(rows_at, part.astype(F32), 0.0).astype(BF16), lane_hot)
        for part in (part0, part1, part2)
    ]
    wd[...] = spread[0] + (spread[1] + spread[2])
    yloc[...] = jnp.broadcast_to(yobs_ref[...].astype(F32), yloc.shape)
    ybuf[1] = yloc[...]

    pl.semaphore_wait(barrier, n + 1)

    copies = []
    w_left = send(wd.at[pl.ds(0, block)], wbuf.at[0], w_ss.at[0], w_rs.at[0], (me, left))
    w_right = send(wd.at[pl.ds(2 * block, block)], wbuf.at[1], w_ss.at[1], w_rs.at[1], (me, right))
    y_up = send(yloc, ybuf.at[0], y_ss.at[0], y_rs.at[0], (peer(1), col))
    y_down = send(yloc, ybuf.at[2], y_ss.at[1], y_rs.at[1], (peer(n - 1), col))

    order = sorted(range(n), key=lambda t: -min(t, n - t))
    obs_copies = []
    for t in order:
        row = peer(t)
        hot = lax.broadcasted_iota(jnp.int32, (cells, width), 0) == idx_ref[pl.ds(row, 1), :]
        hot = jnp.where(hot, 1.0, 0.0).astype(BF16)
        obs_loc[t] = jnp.dot(bgp[row], hot, preferred_element_type=F32).astype(BF16)
        for slot in (0, 1, 2):
            d = (t + 1 - slot) % n
            if d == 0:
                obuf[me, slot] = obs_loc[t]
            else:
                obs_copies.append(
                    send(obs_loc.at[t], obuf.at[me, slot], obs_ss.at[d, slot], obs_rs.at[d, slot], (peer(d), col))
                )
    for copy in obs_copies:
        copy.wait_recv()

    state_copies = []
    for d in range(n - 1, 0, -1):
        state_copies.append(
            send(bgp.at[peer(d)], sbuf.at[me], st_ss.at[d], st_rs.at[d], (peer(d), col))
        )
    sbuf[me] = bgp[me]

    y_up.wait_recv()
    y_down.wait_recv()
    row_id = lax.broadcasted_iota(jnp.int32, (total, 1), 0)
    real = lax.rem(row_id, pad) < m
    for slot in range(3):
        seen = obuf[:, slot].reshape(total, width).astype(F32)
        mean = jnp.sum(seen, axis=0, keepdims=True) / members
        innov = ybuf[slot][0:1, :] - mean
        values = jnp.where(real, seen - mean, jnp.where(row_id == m, innov, 0.0))
        pert[slot] = values.astype(BF16)

    def gram_of(weights):
        acc = None
        for slot in range(3):
            strip_rows = [weights[slot * strips + i:slot * strips + i + 1, :] for i in range(strips)]
            scale = jnp.concatenate(strip_rows, axis=1)
            values = pert[slot]
            weighted = (values.astype(F32) * scale).astype(BF16)
            term = dot_t(weighted, values)
            acc = term if acc is None else acc + term
        return acc

    w_left.wait_recv()
    gsend[0] = gram_of(wbuf[0]).astype(BF16)
    g_right = send(gsend.at[0], grecv.at[0], g_ss.at[0], g_rs.at[0], (me, right))
    w_right.wait_recv()
    gsend[1] = gram_of(wbuf[1]).astype(BF16)
    g_left = send(gsend.at[1], grecv.at[1], g_ss.at[1], g_rs.at[1], (me, left))
    own = gram_of(wd[block:2 * block, :])
    g_right.wait_recv()
    g_left.wait_recv()
    full = own + (grecv[0].astype(F32) + grecv[1].astype(F32))

    col_id = lax.broadcasted_iota(jnp.int32, (1, total), 1)
    real_col = lax.rem(col_id, pad) < m
    same = row_id == col_id
    eye = jnp.where(same, 1.0, 0.0)
    drive = jnp.where(real_col, full[m:m + 1, :], 0.0)
    gram = jnp.where(real & real_col, full, 0.0)
    gram = gram + jnp.where(same & real, (members - 1) / INFLATION, 0.0)
    norm = jnp.sqrt(jnp.sum(jnp.sum(gram * gram, axis=0, keepdims=True), axis=1, keepdims=True))
    root = newton(gram, norm, eye, NS_STEPS)
    inner = jnp.sum(root * drive, axis=1, keepdims=True)
    shift = jnp.sum(root * inner, axis=0, keepdims=True)
    wt[...] = (math.sqrt(members - 1) / jnp.sqrt(norm) * root + shift / norm).astype(BF16)

    for copy in state_copies:
        copy.wait_recv()
    states = sbuf[...].reshape(total, cells).astype(F32)
    state_mean = jnp.sum(states, axis=0, keepdims=True) / members
    state_pert = jnp.where(real, states - state_mean, 0.0).astype(BF16)

    mine = pl.ds(pl.multiple_of(me * cells, 128), cells)
    out_copies = []
    for d in list(range(n - 1, 0, -1)) + [0]:
        dest = peer(d)
        rows = wt[pl.ds(pl.multiple_of(dest * pad, 16), pad), :]
        result = (state_mean + jnp.dot(rows, state_pert, preferred_element_type=F32)).astype(BF16)
        if d == 0:
            out_ref[:, mine] = result
        else:
            oloc[d] = result
            out_copies.append(
                send(oloc.at[d], out_ref.at[:, mine], o_ss.at[d], o_rs.at[d], (dest, col))
            )
    for copy in out_copies:
        copy.wait_recv()
    for copy in obs_copies + state_copies + out_copies:
        copy.wait_send()
    for copy in (w_left, w_right, y_up, y_down, g_right, g_left):
        copy.wait_send()


def local(background, obs_index, yobs, loc_list, loc_count, loc_weight):
    n, regs = lax.axis_size("mem"), lax.axis_size("reg")
    m = background.shape[0]
    rows, width = obs_index.shape[1], obs_index.shape[2]
    cells = background.shape[2] // rows
    length = loc_list.shape[2]
    pad = (m // 16 + 1) * 16
    total = n * pad
    block = -(-3 * (width // 128) // 8) * 8
    vmem = pl.BlockSpec(memory_space=pltpu.VMEM)
    dma = pltpu.SemaphoreType.DMA
    result = pl.pallas_call(
        functools.partial(kernel, n, regs, m, pad, width, cells),
        out_shape=jax.ShapeDtypeStruct((pad, rows * cells), BF16),
        in_specs=[vmem] * 6,
        out_specs=vmem,
        scratch_shapes=[
            pltpu.VMEM((n, pad, cells), BF16),
            pltpu.VMEM((n, pad, width), BF16),
            pltpu.VMEM((n, 3, pad, width), BF16),
            pltpu.VMEM((n, pad, cells), BF16),
            pltpu.VMEM((3 * block, 128), F32),
            pltpu.VMEM((2, block, 128), F32),
            pltpu.VMEM((8, width), F32),
            pltpu.VMEM((3, 8, width), F32),
            pltpu.VMEM((3, total, width), BF16),
            pltpu.VMEM((2, total, total), BF16),
            pltpu.VMEM((2, total, total), BF16),
            pltpu.VMEM((total, total), BF16),
            pltpu.VMEM((n, pad, cells), BF16),
            dma((n, 3)), dma((n, 3)),
            dma((n,)), dma((n,)),
            dma((2,)), dma((2,)),
            dma((2,)), dma((2,)),
            dma((2,)), dma((2,)),
            dma((n,)), dma((n,)),
        ],
        compiler_params=pltpu.CompilerParams(
            collective_id=0, has_side_effects=True, vmem_limit_bytes=40 * 1024 * 1024
        ),
    )(
        background.reshape(m, rows * cells),
        obs_index.reshape(rows, width),
        yobs.reshape(1, width),
        loc_list.reshape(1, length),
        loc_count.reshape(1, 1),
        loc_weight.reshape(1, length),
    )
    return result[:m].reshape(m, 1, rows * cells)


def solution(mesh):
    return jax.shard_map(
        local,
        mesh=mesh,
        in_specs=(
            P("mem", "reg", None),
            P("reg", None, None),
            P("reg", "mem", None),
            P("reg", "mem", None),
            P("reg", "mem"),
            P("reg", "mem", None),
        ),
        out_specs=P("mem", "reg", None),
        check_vma=False,
    )
```

time: 155 us -> 55.4 us (0.36)
  Pallas kernels: 0 us -> 50.4 us
  waiting for transfers between devices: 43.2 us -> 0 us
  local copies, waits for them, and re-layouts: 45.9 us -> 3.94 us
  other arithmetic: 29.8 us -> 0 us
  blocking collectives: 14.6 us -> 0 us
  matrix products: 10.2 us -> 0 us
  starting transfers between devices: 8.95 us -> 0 us
    pallas_call x0 -> x1, Pallas kernels: none -> 50.4 us  [local(): pl.pallas_call(functools.partial(kernel, n, regs, m, pad, width, cells),...]
    ppermute x4 -> x0, waiting for transfers between devices: 29.4 us -> none  [the longest x2 25.4 us: with_halo(): after = lax.ppermute(initial, axis, down)]
    unnamed x1 -> x0, other arithmetic: 22.3 us -> none
    gather x2 -> x0, local copies, waits for them, and re-layouts: 22.1 us -> none  [the longest x1 13.1 us: analyze(): local_innov = jnp.take(innovation, obs_order)]
    all_to_all x1 -> x0, blocking collectives: 14.6 us -> none  [local(): lax.all_to_all(analysis, 'mem', split_axis=0, concat_axis=2, tiled=True)]
    all_to_all x1 -> x0, waiting for transfers between devices: 13.8 us -> none  [local(): lax.all_to_all(background, 'mem', split_axis=2, concat_axis=0, tiled=True)]
    unnamed x18 -> x10, local copies, waits for them, and re-layouts: 14.9 us -> 3.11 us
    dot_general x22 -> x0, matrix products: 10.2 us -> none  [the longest x2 2.74 us: row_products(): lax.dot_general(left_rows, right_rows, (((0,), (0,)), ((), ())), preferre...]
  transfers between devices with their start and end apart: 5 -> 0, of which waited for: 4 -> 0; matrix products, arithmetic and copies ran while one was open for 0% -> 0% of each run, Pallas kernels for 0% -> 0%
where the time goes in v1:
time: 55.4 us; the launch traced here: 55 us
  Pallas kernels  50.4 us (91%)
  local copies, waits for them, and re-layouts  3.94 us (7%)
  between operations  0.69 us (1%)
    pallas_call x1, Pallas kernels, local(): pl.pallas_call(functools.partial(kernel, n, regs, m, pad, width, cells),...  50.4 us
    unnamed x10, local copies, waits for them, and re-layouts  3.11 us

profile of v1, /device:TPU:0, one launch (start us, length us, event | category | flops | bytes accessed | tf_op | source)
XLA Modules:
  0.0 55.0 jit_solution(15747285907679720478)
XLA Ops:
  0.0 0.0 copy-start.1
  0.7 0.0 copy-start.4
  0.7 0.0 copy-done.1
  0.7 0.7 %copy-done.4 = bf16[1,1,512]{2,1,0:T(2,128)(2,1)S(1)} copy-done((bf16[1,1,512]{2,1,0:T(2,128)(2,1)S(1)}, bf16[1,1,512]{2,1,0:T(2,128)(2,1)}, u32[]{:S(2)}) %copy-start.4) | copy-done | bytes 1048
  1.4 0.0 copy-start
  1.4 1.0 %copy-done = bf16[60,1,4096]{2,0,1:T(8,128)(2,1)S(1)} copy-done((bf16[60,1,4096]{2,0,1:T(8,128)(2,1)S(1)}, bf16[60,1,4096]{2,0,1:T(8,128)(2,1)}, u32[]{:S(2)}) %copy-start) | copy-done | bytes 491544
  2.4 0.0 copy-start.2
  2.4 0.7 %copy-done.2 = s32[1,1,2048]{2,1,0:T(1,128)S(1)} copy-done((s32[1,1,2048]{2,1,0:T(1,128)S(1)}, s32[1,1,2048]{2,1,0:T(1,128)}, u32[]{:S(2)}) %copy-start.2) | copy-done | bytes 8216
  3.1 0.0 copy-start.3
  3.1 0.7 %copy-done.3 = f32[1,1,2048]{2,1,0:T(1,128)S(1)} copy-done((f32[1,1,2048]{2,1,0:T(1,128)S(1)}, f32[1,1,2048]{2,1,0:T(1,128)}, u32[]{:S(2)}) %copy-start.3) | copy-done | bytes 8216
  3.8 50.4 %shard_map.64 = bf16[64,4096]{1,0:T(8,128)(2,1)S(1)} custom-call(bf16[60,4096]{1,0:T(8,128)(2,1)S(1)} %bitcast.7, s32[4,512]{1,0:T(4,128)S(1)} %bitcast.8, bf16[1,512]{1,0:T(2,128)(2,1)S(1)} %bitcast.11, s32[1,2048]{1,0:T(1,128)S(1)} %bitcast.9, s32[1,1]{1,0:T(1,128)S(6)} %copy.7.count_ref, f32[1,2048]{1,0:T(1,128)S(1)} %bitcast.10), custom_call_target="tpu_custom_call" | custom-call | tf_op jit(solution)/shard_map/pallas_call | solution.py:230
  54.2 0.8 %slice_bitcast_fusion = bf16[60,1,4096]{2,0,1:T(8,128)(2,1)} fusion(bf16[64,4096]{1,0:T(8,128)(2,1)S(1)} %shard_map.64), kind=kLoop, calls=%fused_computation | loop fusion | bytes 983040 | tf_op jit(solution)/shard_map/reshape | solution.py:267
Async XLA Ops:
  0.0 0.7 %copy-start.1 = (s32[1,4,512]{2,1,0:T(4,128)S(1)}, s32[1,4,512]{2,1,0:T(4,128)}, u32[]{:S(2)}) copy-start(s32[1,4,512]{2,1,0:T(4,128)} %param.7) | copy-start | bytes 24580
  0.7 0.7 %copy-start.4 = (bf16[1,1,512]{2,1,0:T(2,128)(2,1)S(1)}, bf16[1,1,512]{2,1,0:T(2,128)(2,1)}, u32[]{:S(2)}) copy-start(bf16[1,1,512]{2,1,0:T(2,128)(2,1)} %param.8) | copy-start | bytes 3076
  1.4 1.0 %copy-start = (bf16[60,1,4096]{2,0,1:T(8,128)(2,1)S(1)}, bf16[60,1,4096]{2,0,1:T(8,128)(2,1)}, u32[]{:S(2)}) copy-start(bf16[60,1,4096]{2,0,1:T(8,128)(2,1)} %param.6) | copy-start | bytes 1474564
  2.4 0.7 %copy-start.2 = (s32[1,1,2048]{2,1,0:T(1,128)S(1)}, s32[1,1,2048]{2,1,0:T(1,128)}, u32[]{:S(2)}) copy-start(s32[1,1,2048]{2,1,0:T(1,128)} %param.9) | copy-start | bytes 24580
  3.1 0.7 %copy-start.3 = (f32[1,1,2048]{2,1,0:T(1,128)S(1)}, f32[1,1,2048]{2,1,0:T(1,128)}, u32[]{:S(2)}) copy-start(f32[1,1,2048]{2,1,0:T(1,128)} %param.11) | copy-start | bytes 24580

commit v2 on v1

--- a/solution.py
+++ b/solution.py
@@ -53,10 +53,11 @@
 
 def kernel(
     n, regs, m, pad, width, cells,
+    bg_hbm, idx_hbm, yobs_hbm, list_hbm, count_hbm, weight_hbm,
+    out_ref,
     bg_ref, idx_ref, yobs_ref, list_ref, count_ref, weight_ref,
-    out_ref,
     bgp, obs_loc, obuf, sbuf, wd, wbuf, yloc, ybuf, pert, gsend, grecv, wt, oloc,
-    obs_ss, obs_rs, st_ss, st_rs, w_ss, w_rs, y_ss, y_rs, g_ss, g_rs, o_ss, o_rs,
+    obs_ss, obs_rs, st_ss, st_rs, w_ss, w_rs, y_ss, y_rs, g_ss, g_rs, o_ss, o_rs, in_sem,
 ):
     me, col = lax.axis_index("mem"), lax.axis_index("reg")
     left, right = lax.rem(col + regs - 1, regs), lax.rem(col + 1, regs)
@@ -82,10 +83,17 @@
         copy.start()
         return copy
 
-    tail = (m // 16) * 16
-    for q in range(n):
-        bgp[q, tail:pad, :] = jnp.zeros((pad - tail, cells), BF16)
-        bgp[q, 0:m, :] = bg_ref[:, q * cells:(q + 1) * cells]
+    loads = [
+        pltpu.make_async_copy(src, dst, in_sem.at[i])
+        for i, (src, dst) in enumerate((
+            (bg_hbm, bg_ref), (idx_hbm, idx_ref), (yobs_hbm, yobs_ref),
+            (list_hbm, list_ref), (count_hbm, count_ref), (weight_hbm, weight_ref),
+        ))
+    ]
+    for load in loads:
+        load.start()
+    for load in loads[2:]:
+        load.wait()
 
     length = list_ref.shape[1]
     place = lax.broadcasted_iota(jnp.int32, (1, length), 1)
@@ -110,6 +118,13 @@
     yloc[...] = jnp.broadcast_to(yobs_ref[...].astype(F32), yloc.shape)
     ybuf[1] = yloc[...]
 
+    loads[0].wait()
+    loads[1].wait()
+    tail = (m // 16) * 16
+    for q in range(n):
+        bgp[q, tail:pad, :] = jnp.zeros((pad - tail, cells), BF16)
+        bgp[q, 0:m, :] = bg_ref[:, q * cells:(q + 1) * cells]
+
     pl.semaphore_wait(barrier, n + 1)
 
     copies = []
@@ -118,23 +133,85 @@
     y_up = send(yloc, ybuf.at[0], y_ss.at[0], y_rs.at[0], (peer(1), col))
     y_down = send(yloc, ybuf.at[2], y_ss.at[1], y_rs.at[1], (peer(n - 1), col))
 
-    order = sorted(range(n), key=lambda t: -min(t, n - t))
-    obs_copies = []
-    for t in order:
-        row = peer(t)
+    def observe(row):
         hot = lax.broadcasted_iota(jnp.int32, (cells, width), 0) == idx_ref[pl.ds(row, 1), :]
         hot = jnp.where(hot, 1.0, 0.0).astype(BF16)
-        obs_loc[t] = jnp.dot(bgp[row], hot, preferred_element_type=F32).astype(BF16)
-        for slot in (0, 1, 2):
-            d = (t + 1 - slot) % n
-            if d == 0:
-                obuf[me, slot] = obs_loc[t]
-            else:
-                obs_copies.append(
-                    send(obs_loc.at[t], obuf.at[me, slot], obs_ss.at[d, slot], obs_rs.at[d, slot], (peer(d), col))
-                )
-    for copy in obs_copies:
-        copy.wait_recv()
+        return jnp.dot(bgp[row], hot, preferred_element_type=F32).astype(BF16)
+
+    obs_copies = []
+    if n == 4:
+        side = me // 2
+
+        def turn(x, last):
+            return x + side * (last - 2 * x)
+
+        here = turn(me, 3)
+        inner = here == 1
+        other = 1 - here
+
+        def obs_send(row, dest, slot, i):
+            return send(
+                obs_loc.at[row], obuf.at[me, turn(slot, 2)], obs_ss.at[i],
+                obs_rs.at[me, turn(slot, 2)], (turn(dest, 3), col),
+            )
+
+        def landed(source, slot):
+            return pltpu.make_async_remote_copy(
+                src_ref=obs_loc.at[0], dst_ref=obuf.at[turn(source, 3), turn(slot, 2)],
+                send_sem=obs_ss.at[0], recv_sem=obs_rs.at[turn(source, 3), turn(slot, 2)],
+                device_id=(turn(other, 3), col), device_id_type=MESH,
+            )
+
+        for i, (row, dest, slot) in enumerate(((2, 2, 1), (3, 2, 2), (1, 2, 0), (0, 3, 2))):
+            obs_loc[row] = observe(turn(row, 3))
+            obs_copies.append(obs_send(row, dest, slot, i))
+        for slot in range(3):
+            obs_copies.append(obs_send(lax.rem(other + slot + 3, 4), other, slot, 4 + slot))
+        for slot in range(3):
+            obuf[me, turn(slot, 2)] = obs_loc[lax.rem(here + slot + 3, 4)]
+
+        handed = ((2, 1), (2, 0), (3, 1), (3, 0))
+
+        def hand_on(i, source, slot):
+            return pltpu.make_async_remote_copy(
+                src_ref=obuf.at[turn(source, 3), turn(slot, 2)],
+                dst_ref=obuf.at[turn(source, 3), turn(slot + 1, 2)],
+                send_sem=obs_ss.at[7 + i], recv_sem=obs_rs.at[turn(source, 3), turn(slot + 1, 2)],
+                device_id=(turn(0, 3), col), device_id_type=MESH,
+            )
+
+        @pl.when(inner)
+        def _():
+            for i, (source, slot) in enumerate(handed):
+                landed(source, slot).wait_recv()
+                hand_on(i, source, slot).start()
+            for source in (2, 3):
+                landed(source, 2).wait_recv()
+
+        @pl.when(jnp.logical_not(inner))
+        def _():
+            for source in (2, 3):
+                for slot in range(3):
+                    landed(source, slot).wait_recv()
+
+        for slot in range(3):
+            landed(other, slot).wait_recv()
+    else:
+        for t in sorted(range(n), key=lambda t: -min(t, n - t)):
+            obs_loc[t] = observe(peer(t))
+            for slot in (0, 1, 2):
+                d = (t + 1 - slot) % n
+                if d == 0:
+                    obuf[me, slot] = obs_loc[t]
+                else:
+                    obs_copies.append(
+                        send(
+                            obs_loc.at[t], obuf.at[me, slot], obs_ss.at[3 * d + slot],
+                            obs_rs.at[d, slot], (peer(d), col),
+                        )
+                    )
+        for copy in obs_copies:
+            copy.wait_recv()
 
     state_copies = []
     for d in range(n - 1, 0, -1):
@@ -185,8 +262,8 @@
     gram = gram + jnp.where(same & real, (members - 1) / INFLATION, 0.0)
     norm = jnp.sqrt(jnp.sum(jnp.sum(gram * gram, axis=0, keepdims=True), axis=1, keepdims=True))
     root = newton(gram, norm, eye, NS_STEPS)
-    inner = jnp.sum(root * drive, axis=1, keepdims=True)
-    shift = jnp.sum(root * inner, axis=0, keepdims=True)
+    product = jnp.sum(root * drive, axis=1, keepdims=True)
+    shift = jnp.sum(root * product, axis=0, keepdims=True)
     wt[...] = (math.sqrt(members - 1) / jnp.sqrt(norm) * root + shift / norm).astype(BF16)
 
     for copy in state_copies:
@@ -214,6 +291,11 @@
         copy.wait_send()
     for copy in (w_left, w_right, y_up, y_down, g_right, g_left):
         copy.wait_send()
+    if n == 4:
+        @pl.when(inner)
+        def _():
+            for i, (source, slot) in enumerate(handed):
+                hand_on(i, source, slot).wait_send()
 
 
 def local(background, obs_index, yobs, loc_list, loc_count, loc_weight):
@@ -230,9 +312,15 @@
     result = pl.pallas_call(
         functools.partial(kernel, n, regs, m, pad, width, cells),
         out_shape=jax.ShapeDtypeStruct((pad, rows * cells), BF16),
-        in_specs=[vmem] * 6,
+        in_specs=[pl.BlockSpec(memory_space=pltpu.HBM)] * 6,
         out_specs=vmem,
         scratch_shapes=[
+            pltpu.VMEM((m, rows * cells), BF16),
+            pltpu.VMEM((rows, width), jnp.int32),
+            pltpu.VMEM((1, width), BF16),
+            pltpu.VMEM((1, length), jnp.int32),
+            pltpu.VMEM((1, 1), jnp.int32),
+            pltpu.VMEM((1, length), F32),
             pltpu.VMEM((n, pad, cells), BF16),
             pltpu.VMEM((n, pad, width), BF16),
             pltpu.VMEM((n, 3, pad, width), BF16),
@@ -246,12 +334,12 @@
             pltpu.VMEM((2, total, total), BF16),
             pltpu.VMEM((total, total), BF16),
             pltpu.VMEM((n, pad, cells), BF16),
-            dma((n, 3)), dma((n, 3)),
+            dma((3 * n,)), dma((n, 3)),
             dma((n,)), dma((n,)),
             dma((2,)), dma((2,)),
             dma((2,)), dma((2,)),
             dma((2,)), dma((2,)),
-            dma((n,)), dma((n,)),
+            dma((n,)), dma((n,)), dma((6,)),
         ],
         compiler_params=pltpu.CompilerParams(
             collective_id=0, has_side_effects=True, vmem_limit_bytes=40 * 1024 * 1024

time: 55.4 us -> 52.6 us (0.949)
  Pallas kernels: 50.4 us -> 47.6 us
    pallas_call x1, Pallas kernels: 50.4 us -> 47.6 us  [local(): pl.pallas_call(functools.partial(kernel, n, regs, m, pad, width, cells),...]
where the time goes in v2:
time: 52.6 us; the launch traced here: 52.2 us
  Pallas kernels  47.6 us (90%)
  local copies, waits for them, and re-layouts  3.94 us (7%)
  between operations  0.69 us (1%)
    pallas_call x1, Pallas kernels, local(): pl.pallas_call(functools.partial(kernel, n, regs, m, pad, width, cells),...  47.6 us
    unnamed x10, local copies, waits for them, and re-layouts  3.11 us

profile of v2, /device:TPU:0, one launch (start us, length us, event | category | flops | bytes accessed | tf_op | source)
XLA Modules:
  0.0 52.2 jit_solution(10300583468949651214)
XLA Ops:
  0.0 0.0 copy-start.1
  0.7 0.0 copy-start.4
  0.7 0.0 copy-done.1
  0.7 0.7 %copy-done.4 = bf16[1,1,512]{2,1,0:T(2,128)(2,1)S(1)} copy-done((bf16[1,1,512]{2,1,0:T(2,128)(2,1)S(1)}, bf16[1,1,512]{2,1,0:T(2,128)(2,1)}, u32[]{:S(2)}) %copy-start.4) | copy-done | bytes 1048
  1.4 0.0 copy-start
  1.4 1.0 %copy-done = bf16[60,1,4096]{2,0,1:T(8,128)(2,1)S(1)} copy-done((bf16[60,1,4096]{2,0,1:T(8,128)(2,1)S(1)}, bf16[60,1,4096]{2,0,1:T(8,128)(2,1)}, u32[]{:S(2)}) %copy-start) | copy-done | bytes 491544
  2.4 0.0 copy-start.2
  2.4 0.7 %copy-done.2 = s32[1,1,2048]{2,1,0:T(1,128)S(1)} copy-done((s32[1,1,2048]{2,1,0:T(1,128)S(1)}, s32[1,1,2048]{2,1,0:T(1,128)}, u32[]{:S(2)}) %copy-start.2) | copy-done | bytes 8216
  3.1 0.0 copy-start.3
  3.1 0.7 %copy-done.3 = f32[1,1,2048]{2,1,0:T(1,128)S(1)} copy-done((f32[1,1,2048]{2,1,0:T(1,128)S(1)}, f32[1,1,2048]{2,1,0:T(1,128)}, u32[]{:S(2)}) %copy-start.3) | copy-done | bytes 8216
  3.8 47.6 %shard_map.64 = bf16[64,4096]{1,0:T(8,128)(2,1)S(1)} custom-call(bf16[60,4096]{1,0:T(8,128)(2,1)S(1)} %bitcast.7, s32[4,512]{1,0:T(4,128)S(1)} %bitcast.8, bf16[1,512]{1,0:T(2,128)(2,1)S(1)} %bitcast.11, s32[1,2048]{1,0:T(1,128)S(1)} %bitcast.9, s32[1,1]{1,0:T(1,128)S(6)} %copy.7.count_hbm, f32[1,2048]{1,0:T(1,128)S(1)} %bitcast.10), custom_call_target="tpu_custom_call" | custom-call | tf_op jit(solution)/shard_map/pallas_call | solution.py:312
  51.4 0.8 %slice_bitcast_fusion = bf16[60,1,4096]{2,0,1:T(8,128)(2,1)} fusion(bf16[64,4096]{1,0:T(8,128)(2,1)S(1)} %shard_map.64), kind=kLoop, calls=%fused_computation | loop fusion | bytes 983040 | tf_op jit(solution)/shard_map/reshape | solution.py:355
Async XLA Ops:
  0.0 0.7 %copy-start.1 = (s32[1,4,512]{2,1,0:T(4,128)S(1)}, s32[1,4,512]{2,1,0:T(4,128)}, u32[]{:S(2)}) copy-start(s32[1,4,512]{2,1,0:T(4,128)} %param.7) | copy-start | bytes 24580
  0.7 0.7 %copy-start.4 = (bf16[1,1,512]{2,1,0:T(2,128)(2,1)S(1)}, bf16[1,1,512]{2,1,0:T(2,128)(2,1)}, u32[]{:S(2)}) copy-start(bf16[1,1,512]{2,1,0:T(2,128)(2,1)} %param.8) | copy-start | bytes 3076
  1.4 1.0 %copy-start = (bf16[60,1,4096]{2,0,1:T(8,128)(2,1)S(1)}, bf16[60,1,4096]{2,0,1:T(8,128)(2,1)}, u32[]{:S(2)}) copy-start(bf16[60,1,4096]{2,0,1:T(8,128)(2,1)} %param.6) | copy-start | bytes 1474564
  2.4 0.7 %copy-start.2 = (s32[1,1,2048]{2,1,0:T(1,128)S(1)}, s32[1,1,2048]{2,1,0:T(1,128)}, u32[]{:S(2)}) copy-start(s32[1,1,2048]{2,1,0:T(1,128)} %param.9) | copy-start | bytes 24580
  3.1 0.7 %copy-start.3 = (f32[1,1,2048]{2,1,0:T(1,128)S(1)}, f32[1,1,2048]{2,1,0:T(1,128)}, u32[]{:S(2)}) copy-start(f32[1,1,2048]{2,1,0:T(1,128)} %param.11) | copy-start | bytes 24580

commit v3 on v2

--- a/solution.py
+++ b/solution.py
@@ -56,7 +56,7 @@
     bg_hbm, idx_hbm, yobs_hbm, list_hbm, count_hbm, weight_hbm,
     out_ref,
     bg_ref, idx_ref, yobs_ref, list_ref, count_ref, weight_ref,
-    bgp, obs_loc, obuf, sbuf, wd, wbuf, yloc, ybuf, pert, gsend, grecv, wt, oloc,
+    bgp, obs_loc, obuf, sbuf, wd, wbuf, yloc, ybuf, gacc, gsend, grecv, wt, oloc,
     obs_ss, obs_rs, st_ss, st_rs, w_ss, w_rs, y_ss, y_rs, g_ss, g_rs, o_ss, o_rs, in_sem,
 ):
     me, col = lax.axis_index("mem"), lax.axis_index("reg")
@@ -92,9 +92,90 @@
     ]
     for load in loads:
         load.start()
-    for load in loads[2:]:
+
+    for load in loads[:3]:
         load.wait()
-
+    tail = (m // 16) * 16
+    for q in range(n):
+        bgp[q, tail:pad, :] = jnp.zeros((pad - tail, cells), BF16)
+        bgp[q, 0:m, :] = bg_ref[:, q * cells:(q + 1) * cells]
+
+    yloc[...] = jnp.broadcast_to(yobs_ref[...].astype(F32), yloc.shape)
+    ybuf[1] = yloc[...]
+
+
+    pl.semaphore_wait(barrier, n + 1)
+
+    y_up = send(yloc, ybuf.at[0], y_ss.at[0], y_rs.at[0], (peer(1), col))
+    y_down = send(yloc, ybuf.at[2], y_ss.at[1], y_rs.at[1], (peer(n - 1), col))
+
+    def observe(row):
+        hot = lax.broadcasted_iota(jnp.int32, (cells, width), 0) == idx_ref[pl.ds(row, 1), :]
+        hot = jnp.where(hot, 1.0, 0.0).astype(BF16)
+        return jnp.dot(bgp[row], hot, preferred_element_type=F32).astype(BF16)
+
+    obs_copies = []
+    if n == 4:
+        side = me // 2
+
+        def turn(x, last):
+            return x + side * (last - 2 * x)
+
+        here = turn(me, 3)
+        inner = here == 1
+        other = 1 - here
+
+        def obs_send(row, dest, slot, i):
+            return send(
+                obs_loc.at[row], obuf.at[me, turn(slot, 2)], obs_ss.at[i],
+                obs_rs.at[me, turn(slot, 2)], (turn(dest, 3), col),
+            )
+
+        def landed(source, slot):
+            return pltpu.make_async_remote_copy(
+                src_ref=obs_loc.at[0], dst_ref=obuf.at[turn(source, 3), turn(slot, 2)],
+                send_sem=obs_ss.at[0], recv_sem=obs_rs.at[turn(source, 3), turn(slot, 2)],
+                device_id=(turn(other, 3), col), device_id_type=MESH,
+            )
+
+        for i, (row, dest, slot) in enumerate(((2, 2, 1), (3, 2, 2), (1, 2, 0), (0, 3, 2))):
+            obs_loc[row] = observe(turn(row, 3))
+            obs_copies.append(obs_send(row, dest, slot, i))
+        def kth(place, k):
+            return (2 - place, 1 - place, 2 * place)[k]
+
+        for k in range(3):
+            slot = kth(other, k)
+            obs_copies.append(obs_send(lax.rem(other + slot + 3, 4), other, slot, 4 + k))
+        for slot in range(3):
+            obuf[me, turn(slot, 2)] = obs_loc[lax.rem(here + slot + 3, 4)]
+
+        handed = ((2, 1), (2, 0), (3, 1), (3, 0))
+
+        def hand_on(i, source, slot):
+            return pltpu.make_async_remote_copy(
+                src_ref=obuf.at[turn(source, 3), turn(slot, 2)],
+                dst_ref=obuf.at[turn(source, 3), turn(slot + 1, 2)],
+                send_sem=obs_ss.at[7 + i], recv_sem=obs_rs.at[turn(source, 3), turn(slot + 1, 2)],
+                device_id=(turn(0, 3), col), device_id_type=MESH,
+            )
+    else:
+        for t in sorted(range(n), key=lambda t: -min(t, n - t)):
+            obs_loc[t] = observe(peer(t))
+            for slot in (0, 1, 2):
+                d = (t + 1 - slot) % n
+                if d == 0:
+                    obuf[me, slot] = obs_loc[t]
+                else:
+                    obs_copies.append(
+                        send(
+                            obs_loc.at[t], obuf.at[me, slot], obs_ss.at[3 * d + slot],
+                            obs_rs.at[d, slot], (peer(d), col),
+                        )
+                    )
+
+    for load in loads[3:]:
+        load.wait()
     length = list_ref.shape[1]
     place = lax.broadcasted_iota(jnp.int32, (1, length), 1)
     live = jnp.where(place < count_ref[...], weight_ref[...], 0.0)
@@ -115,103 +196,62 @@
         for part in (part0, part1, part2)
     ]
     wd[...] = spread[0] + (spread[1] + spread[2])
-    yloc[...] = jnp.broadcast_to(yobs_ref[...].astype(F32), yloc.shape)
-    ybuf[1] = yloc[...]
-
-    loads[0].wait()
-    loads[1].wait()
-    tail = (m // 16) * 16
-    for q in range(n):
-        bgp[q, tail:pad, :] = jnp.zeros((pad - tail, cells), BF16)
-        bgp[q, 0:m, :] = bg_ref[:, q * cells:(q + 1) * cells]
-
-    pl.semaphore_wait(barrier, n + 1)
-
-    copies = []
     w_left = send(wd.at[pl.ds(0, block)], wbuf.at[0], w_ss.at[0], w_rs.at[0], (me, left))
     w_right = send(wd.at[pl.ds(2 * block, block)], wbuf.at[1], w_ss.at[1], w_rs.at[1], (me, right))
-    y_up = send(yloc, ybuf.at[0], y_ss.at[0], y_rs.at[0], (peer(1), col))
-    y_down = send(yloc, ybuf.at[2], y_ss.at[1], y_rs.at[1], (peer(n - 1), col))
-
-    def observe(row):
-        hot = lax.broadcasted_iota(jnp.int32, (cells, width), 0) == idx_ref[pl.ds(row, 1), :]
-        hot = jnp.where(hot, 1.0, 0.0).astype(BF16)
-        return jnp.dot(bgp[row], hot, preferred_element_type=F32).astype(BF16)
-
-    obs_copies = []
+
     if n == 4:
-        side = me // 2
-
-        def turn(x, last):
-            return x + side * (last - 2 * x)
-
-        here = turn(me, 3)
-        inner = here == 1
-        other = 1 - here
-
-        def obs_send(row, dest, slot, i):
-            return send(
-                obs_loc.at[row], obuf.at[me, turn(slot, 2)], obs_ss.at[i],
-                obs_rs.at[me, turn(slot, 2)], (turn(dest, 3), col),
-            )
-
-        def landed(source, slot):
-            return pltpu.make_async_remote_copy(
-                src_ref=obs_loc.at[0], dst_ref=obuf.at[turn(source, 3), turn(slot, 2)],
-                send_sem=obs_ss.at[0], recv_sem=obs_rs.at[turn(source, 3), turn(slot, 2)],
-                device_id=(turn(other, 3), col), device_id_type=MESH,
-            )
-
-        for i, (row, dest, slot) in enumerate(((2, 2, 1), (3, 2, 2), (1, 2, 0), (0, 3, 2))):
-            obs_loc[row] = observe(turn(row, 3))
-            obs_copies.append(obs_send(row, dest, slot, i))
-        for slot in range(3):
-            obs_copies.append(obs_send(lax.rem(other + slot + 3, 4), other, slot, 4 + slot))
-        for slot in range(3):
-            obuf[me, turn(slot, 2)] = obs_loc[lax.rem(here + slot + 3, 4)]
-
-        handed = ((2, 1), (2, 0), (3, 1), (3, 0))
-
-        def hand_on(i, source, slot):
-            return pltpu.make_async_remote_copy(
-                src_ref=obuf.at[turn(source, 3), turn(slot, 2)],
-                dst_ref=obuf.at[turn(source, 3), turn(slot + 1, 2)],
-                send_sem=obs_ss.at[7 + i], recv_sem=obs_rs.at[turn(source, 3), turn(slot + 1, 2)],
-                device_id=(turn(0, 3), col), device_id_type=MESH,
-            )
-
         @pl.when(inner)
         def _():
             for i, (source, slot) in enumerate(handed):
                 landed(source, slot).wait_recv()
                 hand_on(i, source, slot).start()
+
+    def take(k):
+        if n != 4:
+            if k == 0:
+                for copy in obs_copies:
+                    copy.wait_recv()
+            return k
+        slot = kth(here, k)
+        if k == 2:
             for source in (2, 3):
-                landed(source, 2).wait_recv()
-
-        @pl.when(jnp.logical_not(inner))
-        def _():
-            for source in (2, 3):
-                for slot in range(3):
+                landed(source, slot).wait_recv()
+        else:
+            @pl.when(jnp.logical_not(inner))
+            def _():
+                for source in (2, 3):
                     landed(source, slot).wait_recv()
-
-        for slot in range(3):
-            landed(other, slot).wait_recv()
-    else:
-        for t in sorted(range(n), key=lambda t: -min(t, n - t)):
-            obs_loc[t] = observe(peer(t))
-            for slot in (0, 1, 2):
-                d = (t + 1 - slot) % n
-                if d == 0:
-                    obuf[me, slot] = obs_loc[t]
-                else:
-                    obs_copies.append(
-                        send(
-                            obs_loc.at[t], obuf.at[me, slot], obs_ss.at[3 * d + slot],
-                            obs_rs.at[d, slot], (peer(d), col),
-                        )
-                    )
-        for copy in obs_copies:
-            copy.wait_recv()
+        landed(other, slot).wait_recv()
+        return turn(slot, 2)
+
+    row_id = lax.broadcasted_iota(jnp.int32, (total, 1), 0)
+    real = lax.rem(row_id, pad) < m
+
+    def perturbed(slot):
+        seen = obuf[:, slot].reshape(total, width).astype(F32)
+        mean = jnp.sum(seen, axis=0, keepdims=True) / members
+        innov = ybuf[slot][0:1, :] - mean
+        values = jnp.where(real, seen - mean, jnp.where(row_id == m, innov, 0.0))
+        return values.astype(BF16)
+
+    def term(values, weights, slot):
+        strip_rows = [weights[pl.ds(slot * strips + i, 1), :] for i in range(strips)]
+        scale = jnp.concatenate(strip_rows, axis=1)
+        return dot_t((values.astype(F32) * scale).astype(BF16), values)
+
+    tables = (wbuf.at[0], wbuf.at[1], wd.at[pl.ds(block, block)])
+    for k in range(2):
+        slot = take(k)
+        if k == 0:
+            for copy in (y_up, y_down, w_left, w_right):
+                copy.wait_recv()
+        values = perturbed(slot)
+        for i, table in enumerate(tables):
+            if k == 0:
+                gacc[i] = term(values, table, slot)
+            else:
+                gacc[i] += term(values, table, slot)
+    slot = take(2)
 
     state_copies = []
     for d in range(n - 1, 0, -1):
@@ -220,35 +260,12 @@
         )
     sbuf[me] = bgp[me]
 
-    y_up.wait_recv()
-    y_down.wait_recv()
-    row_id = lax.broadcasted_iota(jnp.int32, (total, 1), 0)
-    real = lax.rem(row_id, pad) < m
-    for slot in range(3):
-        seen = obuf[:, slot].reshape(total, width).astype(F32)
-        mean = jnp.sum(seen, axis=0, keepdims=True) / members
-        innov = ybuf[slot][0:1, :] - mean
-        values = jnp.where(real, seen - mean, jnp.where(row_id == m, innov, 0.0))
-        pert[slot] = values.astype(BF16)
-
-    def gram_of(weights):
-        acc = None
-        for slot in range(3):
-            strip_rows = [weights[slot * strips + i:slot * strips + i + 1, :] for i in range(strips)]
-            scale = jnp.concatenate(strip_rows, axis=1)
-            values = pert[slot]
-            weighted = (values.astype(F32) * scale).astype(BF16)
-            term = dot_t(weighted, values)
-            acc = term if acc is None else acc + term
-        return acc
-
-    w_left.wait_recv()
-    gsend[0] = gram_of(wbuf[0]).astype(BF16)
+    values = perturbed(slot)
+    gsend[0] = (gacc[0] + term(values, tables[0], slot)).astype(BF16)
     g_right = send(gsend.at[0], grecv.at[0], g_ss.at[0], g_rs.at[0], (me, right))
-    w_right.wait_recv()
-    gsend[1] = gram_of(wbuf[1]).astype(BF16)
+    gsend[1] = (gacc[1] + term(values, tables[1], slot)).astype(BF16)
     g_left = send(gsend.at[1], grecv.at[1], g_ss.at[1], g_rs.at[1], (me, left))
-    own = gram_of(wd[block:2 * block, :])
+    own = gacc[2] + term(values, tables[2], slot)
     g_right.wait_recv()
     g_left.wait_recv()
     full = own + (grecv[0].astype(F32) + grecv[1].astype(F32))
@@ -329,7 +346,7 @@
             pltpu.VMEM((2, block, 128), F32),
             pltpu.VMEM((8, width), F32),
             pltpu.VMEM((3, 8, width), F32),
-            pltpu.VMEM((3, total, width), BF16),
+            pltpu.VMEM((3, total, total), F32),
             pltpu.VMEM((2, total, total), BF16),
             pltpu.VMEM((2, total, total), BF16),
             pltpu.VMEM((total, total), BF16),
@@ -342,7 +359,7 @@
             dma((n,)), dma((n,)), dma((6,)),
         ],
         compiler_params=pltpu.CompilerParams(
-            collective_id=0, has_side_effects=True, vmem_limit_bytes=40 * 1024 * 1024
+            collective_id=0, has_side_effects=True
         ),
     )(
         background.reshape(m, rows * cells),

time: 52.6 us -> 51 us (0.970)
  local copies, waits for them, and re-layouts: 3.94 us -> 1.87 us
  Pallas kernels: 47.6 us -> 48.2 us
    unnamed x10 -> x0, local copies, waits for them, and re-layouts: 3.11 us -> none
    reshape x1, local copies, waits for them, and re-layouts: 0.83 us -> 1.87 us  [local(): return result[:m].reshape(m, 1, rows * cells)]
    pallas_call x1, Pallas kernels: 47.6 us -> 48.2 us  [local(): pl.pallas_call(functools.partial(kernel, n, regs, m, pad, width, cells),...]
where the time goes in v3:
time: 51 us; the launch traced here: 50.8 us
  Pallas kernels  48.2 us (95%)
  local copies, waits for them, and re-layouts  1.87 us (4%)
  between operations  0.66 us (1%)
    pallas_call x1, Pallas kernels, local(): pl.pallas_call(functools.partial(kernel, n, regs, m, pad, width, cells),...  48.2 us
    reshape x1, local copies, waits for them, and re-layouts, local(): return result[:m].reshape(m, 1, rows * cells)  1.87 us

profile of v3, /device:TPU:0, one launch (start us, length us, event | category | flops | bytes accessed | tf_op | source)
XLA Modules:
  0.0 50.8 jit_solution(7388400758223078815)
XLA Ops:
  0.7 48.2 %shard_map.64 = bf16[64,4096]{1,0:T(8,128)(2,1)} custom-call(bf16[60,4096]{1,0:T(8,128)(2,1)} %bitcast.7, s32[4,512]{1,0:T(4,128)} %bitcast.8, bf16[1,512]{1,0:T(2,128)(2,1)} %bitcast.11, s32[1,2048]{1,0:T(1,128)} %bitcast.9, s32[1,1]{1,0:T(1,128)S(6)} %copy.7.count_hbm, f32[1,2048]{1,0:T(1,128)} %bitcast.10), custom_call_target="tpu_custom_call" | custom-call | tf_op jit(solution)/shard_map/pallas_call | solution.py:329
  48.9 1.9 %slice_bitcast_fusion = bf16[60,1,4096]{2,0,1:T(8,128)(2,1)} fusion(bf16[64,4096]{1,0:T(8,128)(2,1)} %shard_map.64), kind=kLoop, calls=%fused_computation | loop fusion | bytes 983040 | tf_op jit(solution)/shard_map/reshape | solution.py:372

commit v4 on v3

--- a/solution.py
+++ b/solution.py
@@ -56,7 +56,7 @@
     bg_hbm, idx_hbm, yobs_hbm, list_hbm, count_hbm, weight_hbm,
     out_ref,
     bg_ref, idx_ref, yobs_ref, list_ref, count_ref, weight_ref,
-    bgp, obs_loc, obuf, sbuf, wd, wbuf, yloc, ybuf, gacc, gsend, grecv, wt, oloc,
+    bgp, obs_loc, obuf, sbuf, wd, wbuf, yloc, ybuf, gacc, gsend, grecv, wt, oloc, oland,
     obs_ss, obs_rs, st_ss, st_rs, w_ss, w_rs, y_ss, y_rs, g_ss, g_rs, o_ss, o_rs, in_sem,
 ):
     me, col = lax.axis_index("mem"), lax.axis_index("reg")
@@ -102,7 +102,6 @@
 
     yloc[...] = jnp.broadcast_to(yobs_ref[...].astype(F32), yloc.shape)
     ybuf[1] = yloc[...]
-
 
     pl.semaphore_wait(barrier, n + 1)
 
@@ -199,6 +198,17 @@
     w_left = send(wd.at[pl.ds(0, block)], wbuf.at[0], w_ss.at[0], w_rs.at[0], (me, left))
     w_right = send(wd.at[pl.ds(2 * block, block)], wbuf.at[1], w_ss.at[1], w_rs.at[1], (me, right))
 
+    def state_send(dest, i):
+        return send(bgp.at[dest], sbuf.at[me], st_ss.at[i], st_rs.at[me], (dest, col))
+
+    sbuf[me] = bgp[me]
+    if n == 4:
+        state_copies = [state_send(turn(2, 3), 0)]
+        state_later = [turn(3, 3), turn(other, 3)]
+    else:
+        state_copies = []
+        state_later = [peer(d) for d in range(n - 1, 0, -1)]
+
     if n == 4:
         @pl.when(inner)
         def _():
@@ -251,14 +261,10 @@
                 gacc[i] = term(values, table, slot)
             else:
                 gacc[i] += term(values, table, slot)
+        if k == 0:
+            for dest in state_later:
+                state_copies.append(state_send(dest, len(state_copies)))
     slot = take(2)
-
-    state_copies = []
-    for d in range(n - 1, 0, -1):
-        state_copies.append(
-            send(bgp.at[peer(d)], sbuf.at[me], st_ss.at[d], st_rs.at[d], (peer(d), col))
-        )
-    sbuf[me] = bgp[me]
 
     values = perturbed(slot)
     gsend[0] = (gacc[0] + term(values, tables[0], slot)).astype(BF16)
@@ -283,27 +289,35 @@
     shift = jnp.sum(root * product, axis=0, keepdims=True)
     wt[...] = (math.sqrt(members - 1) / jnp.sqrt(norm) * root + shift / norm).astype(BF16)
 
-    for copy in state_copies:
-        copy.wait_recv()
+    for d in range(1, n):
+        pltpu.make_async_remote_copy(
+            src_ref=bgp.at[0], dst_ref=sbuf.at[peer(d)], send_sem=st_ss.at[0], recv_sem=st_rs.at[peer(d)],
+            device_id=(peer(d), col), device_id_type=MESH,
+        ).wait_recv()
     states = sbuf[...].reshape(total, cells).astype(F32)
     state_mean = jnp.sum(states, axis=0, keepdims=True) / members
     state_pert = jnp.where(real, states - state_mean, 0.0).astype(BF16)
 
-    mine = pl.ds(pl.multiple_of(me * cells, 128), cells)
     out_copies = []
     for d in list(range(n - 1, 0, -1)) + [0]:
         dest = peer(d)
         rows = wt[pl.ds(pl.multiple_of(dest * pad, 16), pad), :]
         result = (state_mean + jnp.dot(rows, state_pert, preferred_element_type=F32)).astype(BF16)
         if d == 0:
-            out_ref[:, mine] = result
+            oland[me] = result
         else:
             oloc[d] = result
             out_copies.append(
-                send(oloc.at[d], out_ref.at[:, mine], o_ss.at[d], o_rs.at[d], (dest, col))
+                send(oloc.at[d], oland.at[me], o_ss.at[d], o_rs.at[d], (dest, col))
             )
-    for copy in out_copies:
+
+    def finish(source):
+        out_ref[:, pl.ds(pl.multiple_of(source * cells, 128), cells)] = oland[source, 0:m, :]
+
+    finish(me)
+    for d, copy in reversed(list(zip(range(n - 1, 0, -1), out_copies))):
         copy.wait_recv()
+        finish(peer(n - d))
     for copy in obs_copies + state_copies + out_copies:
         copy.wait_send()
     for copy in (w_left, w_right, y_up, y_down, g_right, g_left):
@@ -328,7 +342,7 @@
     dma = pltpu.SemaphoreType.DMA
     result = pl.pallas_call(
         functools.partial(kernel, n, regs, m, pad, width, cells),
-        out_shape=jax.ShapeDtypeStruct((pad, rows * cells), BF16),
+        out_shape=jax.ShapeDtypeStruct((m, rows * cells), BF16),
         in_specs=[pl.BlockSpec(memory_space=pltpu.HBM)] * 6,
         out_specs=vmem,
         scratch_shapes=[
@@ -351,6 +365,7 @@
             pltpu.VMEM((2, total, total), BF16),
             pltpu.VMEM((total, total), BF16),
             pltpu.VMEM((n, pad, cells), BF16),
+            pltpu.VMEM((n, pad, cells), BF16),
             dma((3 * n,)), dma((n, 3)),
             dma((n,)), dma((n,)),
             dma((2,)), dma((2,)),
@@ -369,7 +384,7 @@
         loc_count.reshape(1, 1),
         loc_weight.reshape(1, length),
     )
-    return result[:m].reshape(m, 1, rows * cells)
+    return result.reshape(m, 1, rows * cells)
 
 
 def solution(mesh):

time: 51 us -> 48.9 us (0.959)
  Pallas kernels: 48.2 us -> 45.8 us
    pallas_call x1, Pallas kernels: 48.2 us -> 45.8 us  [local(): pl.pallas_call(functools.partial(kernel, n, regs, m, pad, width, cells),...]
    reshape x1 -> x0, local copies, waits for them, and re-layouts: 1.87 us -> none  [local(): return result[:m].reshape(m, 1, rows * cells)]
    unnamed x0 -> x1, local copies, waits for them, and re-layouts: none -> 1.87 us
where the time goes in v4:
time: 48.9 us; the launch traced here: 48.3 us
  Pallas kernels  45.8 us (94%)
  local copies, waits for them, and re-layouts  1.87 us (4%)
  between operations  0.66 us (1%)
    pallas_call x1, Pallas kernels, local(): pl.pallas_call(functools.partial(kernel, n, regs, m, pad, width, cells),...  45.8 us
    unnamed x1, local copies, waits for them, and re-layouts  1.87 us

profile of v4, /device:TPU:0, one launch (start us, length us, event | category | flops | bytes accessed | tf_op | source)
XLA Modules:
  0.0 48.3 jit_solution(5568631531983716450)
XLA Ops:
  0.7 45.8 %shard_map.64 = bf16[60,4096]{1,0:T(8,128)(2,1)} custom-call(bf16[60,4096]{1,0:T(8,128)(2,1)} %bitcast.7, s32[4,512]{1,0:T(4,128)} %bitcast.8, bf16[1,512]{1,0:T(2,128)(2,1)} %bitcast.11, s32[1,2048]{1,0:T(1,128)} %bitcast.9, s32[1,1]{1,0:T(1,128)S(6)} %copy.8.count_hbm, f32[1,2048]{1,0:T(1,128)} %bitcast.10), custom_call_target="tpu_custom_call" | custom-call | tf_op jit(solution)/shard_map/pallas_call | solution.py:343
  46.4 1.9 %copy.9 = bf16[60,1,4096]{2,0,1:T(8,128)(2,1)} copy(bf16[60,1,4096]{2,0,1:T(8,128)(2,1)} %bitcast.6) | data formatting | bytes 983040

commit v5 on v4

--- a/solution.py
+++ b/solution.py
@@ -20,11 +20,14 @@
     return high, (x - high.astype(F32)).astype(BF16)
 
 
-def mm(a, b):
+def mm(a, b, passes):
+    top = jnp.dot(a[0], b[0], preferred_element_type=F32)
+    if passes == 1:
+        return top
     return (
         jnp.dot(a[0], b[1], preferred_element_type=F32)
         + jnp.dot(a[1], b[0], preferred_element_type=F32)
-        + jnp.dot(a[0], b[0], preferred_element_type=F32)
+        + top
     )
 
 
@@ -33,29 +36,26 @@
 
 
 def newton(gram, norm, eye, steps):
-    current = gram * (1.0 / norm)
+    t = gram * (1.0 / norm)
     root = None
     for step in range(steps):
-        last = step == steps - 1
+        passes = 1 if step < steps - 2 else 3
+        t_s = split(t)
         if root is None:
-            corr = 1.5 * eye - 0.5 * current
-            corr_s = split(corr)
-            root = corr
+            root = 1.5 * eye - 0.5 * t
         else:
-            cur_s, root_s = split(current), split(root)
-            corr = 1.5 * eye - 0.5 * mm(root_s, cur_s)
-            corr_s = split(corr)
-            root = mm(corr_s, root_s)
-        if not last:
-            current = mm(split(current), corr_s)
+            root = 1.5 * root - 0.5 * mm(t_s, split(root), passes)
+        if step < steps - 1:
+            square = mm(t_s, t_s, passes)
+            t = 2.25 * t - 1.5 * square + 0.25 * mm(t_s, split(square), passes)
     return root
 
 
 def kernel(
     n, regs, m, pad, width, cells,
-    bg_hbm, idx_hbm, yobs_hbm, list_hbm, count_hbm, weight_hbm,
+    bg_hbm, idx_hbm, yobs_hbm, list_hbm, weight_hbm, count_ref,
     out_ref,
-    bg_ref, idx_ref, yobs_ref, list_ref, count_ref, weight_ref,
+    bg_ref, idx_ref, yobs_ref, list_ref, weight_ref,
     bgp, obs_loc, obuf, sbuf, wd, wbuf, yloc, ybuf, gacc, gsend, grecv, wt, oloc, oland,
     obs_ss, obs_rs, st_ss, st_rs, w_ss, w_rs, y_ss, y_rs, g_ss, g_rs, o_ss, o_rs, in_sem,
 ):
@@ -87,7 +87,7 @@
         pltpu.make_async_copy(src, dst, in_sem.at[i])
         for i, (src, dst) in enumerate((
             (bg_hbm, bg_ref), (idx_hbm, idx_ref), (yobs_hbm, yobs_ref),
-            (list_hbm, list_ref), (count_hbm, count_ref), (weight_hbm, weight_ref),
+            (list_hbm, list_ref), (weight_hbm, weight_ref),
         ))
     ]
     for load in loads:
@@ -177,7 +177,7 @@
         load.wait()
     length = list_ref.shape[1]
     place = lax.broadcasted_iota(jnp.int32, (1, length), 1)
-    live = jnp.where(place < count_ref[...], weight_ref[...], 0.0)
+    live = jnp.where(place < count_ref[0, 0], weight_ref[...], 0.0)
     part0 = live.astype(BF16)
     rest = live - part0.astype(F32)
     part1 = rest.astype(BF16)
@@ -299,25 +299,31 @@
     state_pert = jnp.where(real, states - state_mean, 0.0).astype(BF16)
 
     out_copies = []
-    for d in list(range(n - 1, 0, -1)) + [0]:
-        dest = peer(d)
+    if n == 4:
+        dests = [turn(3, 3), turn(2, 3), turn(other, 3)]
+    else:
+        dests = [peer(d) for d in range(n - 1, 0, -1)]
+    for d, dest in enumerate(dests + [me]):
         rows = wt[pl.ds(pl.multiple_of(dest * pad, 16), pad), :]
         result = (state_mean + jnp.dot(rows, state_pert, preferred_element_type=F32)).astype(BF16)
-        if d == 0:
+        if d == n - 1:
             oland[me] = result
         else:
             oloc[d] = result
             out_copies.append(
-                send(oloc.at[d], oland.at[me], o_ss.at[d], o_rs.at[d], (dest, col))
+                send(oloc.at[d], oland.at[me], o_ss.at[d], o_rs.at[me], (dest, col))
             )
 
     def finish(source):
         out_ref[:, pl.ds(pl.multiple_of(source * cells, 128), cells)] = oland[source, 0:m, :]
 
     finish(me)
-    for d, copy in reversed(list(zip(range(n - 1, 0, -1), out_copies))):
-        copy.wait_recv()
-        finish(peer(n - d))
+    for source in reversed(dests):
+        pltpu.make_async_remote_copy(
+            src_ref=oloc.at[0], dst_ref=oland.at[source], send_sem=o_ss.at[0], recv_sem=o_rs.at[source],
+            device_id=(source, col), device_id_type=MESH,
+        ).wait_recv()
+        finish(source)
     for copy in obs_copies + state_copies + out_copies:
         copy.wait_send()
     for copy in (w_left, w_right, y_up, y_down, g_right, g_left):
@@ -343,14 +349,13 @@
     result = pl.pallas_call(
         functools.partial(kernel, n, regs, m, pad, width, cells),
         out_shape=jax.ShapeDtypeStruct((m, rows * cells), BF16),
-        in_specs=[pl.BlockSpec(memory_space=pltpu.HBM)] * 6,
+        in_specs=[pl.BlockSpec(memory_space=pltpu.HBM)] * 5 + [pl.BlockSpec(memory_space=pltpu.SMEM)],
         out_specs=vmem,
         scratch_shapes=[
             pltpu.VMEM((m, rows * cells), BF16),
             pltpu.VMEM((rows, width), jnp.int32),
             pltpu.VMEM((1, width), BF16),
             pltpu.VMEM((1, length), jnp.int32),
-            pltpu.VMEM((1, 1), jnp.int32),
             pltpu.VMEM((1, length), F32),
             pltpu.VMEM((n, pad, cells), BF16),
             pltpu.VMEM((n, pad, width), BF16),
@@ -371,18 +376,23 @@
             dma((2,)), dma((2,)),
             dma((2,)), dma((2,)),
             dma((2,)), dma((2,)),
-            dma((n,)), dma((n,)), dma((6,)),
+            dma((n,)), dma((n,)), dma((5,)),
         ],
         compiler_params=pltpu.CompilerParams(
-            collective_id=0, has_side_effects=True
+            collective_id=0, has_side_effects=True, vmem_limit_bytes=40 * 1024 * 1024
         ),
     )(
-        background.reshape(m, rows * cells),
-        obs_index.reshape(rows, width),
-        yobs.reshape(1, width),
-        loc_list.reshape(1, length),
+        *(
+            pltpu.with_memory_space_constraint(x, pltpu.HBM)
+            for x in (
+                background.reshape(m, rows * cells),
+                obs_index.reshape(rows, width),
+                yobs.reshape(1, width),
+                loc_list.reshape(1, length),
+                loc_weight.reshape(1, length),
+            )
+        ),
         loc_count.reshape(1, 1),
-        loc_weight.reshape(1, length),
     )
     return result.reshape(m, 1, rows * cells)
 

time: 48.9 us -> 44.7 us (0.914)
  Pallas kernels: 45.8 us -> 43.1 us
  local copies, waits for them, and re-layouts: 1.87 us -> 0.8 us
    pallas_call x1, Pallas kernels: 45.8 us -> 43.1 us  [local(): pl.pallas_call(functools.partial(kernel, n, regs, m, pad, width, cells),...]
    unnamed x1, local copies, waits for them, and re-layouts: 1.87 us -> 0.8 us
where the time goes in v5:
time: 44.7 us; the launch traced here: 44.5 us
  Pallas kernels  43.1 us (96%)
  local copies, waits for them, and re-layouts  0.8 us (2%)
  between operations  0.66 us (1%)
    pallas_call x1, Pallas kernels, local(): pl.pallas_call(functools.partial(kernel, n, regs, m, pad, width, cells),...  43.1 us

profile of v5, /device:TPU:0, one launch (start us, length us, event | category | flops | bytes accessed | tf_op | source)
XLA Modules:
  0.0 44.5 jit_solution(5985557386006900406)
XLA Ops:
  0.7 43.1 %shard_map.64 = bf16[60,4096]{1,0:T(8,128)(2,1)S(1)} custom-call(bf16[60,4096]{1,0:T(8,128)(2,1)} %bitcast.7, s32[4,512]{1,0:T(4,128)} %bitcast.8, bf16[1,512]{1,0:T(2,128)(2,1)} %bitcast.11, s32[1,2048]{1,0:T(1,128)} %bitcast.9, f32[1,2048]{1,0:T(1,128)} %bitcast.10, s32[1,1]{1,0:T(1,128)S(6)} %copy.8.count_ref), custom_call_target="tpu_custom_call" | custom-call | tf_op jit(solution)/shard_map/pallas_call | solution.py:349
  43.7 0.8 %copy.9 = bf16[60,1,4096]{2,0,1:T(8,128)(2,1)} copy(bf16[60,1,4096]{2,0,1:T(8,128)(2,1)S(1)} %bitcast.6) | data formatting | bytes 983040

commit v6 on v5

--- a/solution.py
+++ b/solution.py
@@ -51,12 +51,39 @@
     return root
 
 
+def packed_shape(m, pad, width):
+    rest = m % 16
+    base = m - rest
+    if rest and base and base % rest == 0 and (width * rest // base) % 128 == 0 and width * rest % base == 0:
+        return base, width + width * rest // base
+    return pad, width
+
+
+def pack(x, m, shape):
+    base, lanes = shape
+    width = x.shape[1]
+    if lanes == width:
+        return x.astype(BF16)
+    extra = lanes - width
+    rest = jnp.concatenate([x[base:m, i:i + extra] for i in range(0, width, extra)], axis=0)
+    return jnp.concatenate([x[:base], rest], axis=1).astype(BF16)
+
+
+def unpack(y, m, pad, width):
+    y = y.astype(F32)
+    if y.shape[1] == width:
+        return y
+    rest = m - y.shape[0]
+    tail = jnp.concatenate([y[i:i + rest, width:] for i in range(0, y.shape[0], rest)], axis=1)
+    return jnp.concatenate([y[:, :width], tail, jnp.zeros((pad - m, width), F32)], axis=0)
+
+
 def kernel(
     n, regs, m, pad, width, cells,
     bg_hbm, idx_hbm, yobs_hbm, list_hbm, weight_hbm, count_ref,
     out_ref,
     bg_ref, idx_ref, yobs_ref, list_ref, weight_ref,
-    bgp, obs_loc, obuf, sbuf, wd, wbuf, yloc, ybuf, gacc, gsend, grecv, wt, oloc, oland,
+    bgp, spack, obs_loc, obuf, sbuf, wd, wbuf, yloc, ybuf, gacc, gsend, grecv, wt, oloc, oland,
     obs_ss, obs_rs, st_ss, st_rs, w_ss, w_rs, y_ss, y_rs, g_ss, g_rs, o_ss, o_rs, in_sem,
 ):
     me, col = lax.axis_index("mem"), lax.axis_index("reg")
@@ -111,7 +138,8 @@
     def observe(row):
         hot = lax.broadcasted_iota(jnp.int32, (cells, width), 0) == idx_ref[pl.ds(row, 1), :]
         hot = jnp.where(hot, 1.0, 0.0).astype(BF16)
-        return jnp.dot(bgp[row], hot, preferred_element_type=F32).astype(BF16)
+        seen = jnp.dot(bgp[row], hot, preferred_element_type=F32)
+        return pack(seen, m, obs_loc.shape[1:])
 
     obs_copies = []
     if n == 4:
@@ -199,9 +227,11 @@
     w_right = send(wd.at[pl.ds(2 * block, block)], wbuf.at[1], w_ss.at[1], w_rs.at[1], (me, right))
 
     def state_send(dest, i):
-        return send(bgp.at[dest], sbuf.at[me], st_ss.at[i], st_rs.at[me], (dest, col))
-
-    sbuf[me] = bgp[me]
+        return send(spack.at[dest], sbuf.at[me], st_ss.at[i], st_rs.at[me], (dest, col))
+
+    for q in range(n):
+        spack[q] = pack(bgp[q].astype(F32), m, spack.shape[1:])
+    sbuf[me] = spack[me]
     if n == 4:
         state_copies = [state_send(turn(2, 3), 0)]
         state_later = [turn(3, 3), turn(other, 3)]
@@ -238,7 +268,7 @@
     real = lax.rem(row_id, pad) < m
 
     def perturbed(slot):
-        seen = obuf[:, slot].reshape(total, width).astype(F32)
+        seen = jnp.concatenate([unpack(obuf[z, slot], m, pad, width) for z in range(n)], axis=0)
         mean = jnp.sum(seen, axis=0, keepdims=True) / members
         innov = ybuf[slot][0:1, :] - mean
         values = jnp.where(real, seen - mean, jnp.where(row_id == m, innov, 0.0))
@@ -291,10 +321,10 @@
 
     for d in range(1, n):
         pltpu.make_async_remote_copy(
-            src_ref=bgp.at[0], dst_ref=sbuf.at[peer(d)], send_sem=st_ss.at[0], recv_sem=st_rs.at[peer(d)],
+            src_ref=spack.at[0], dst_ref=sbuf.at[peer(d)], send_sem=st_ss.at[0], recv_sem=st_rs.at[peer(d)],
             device_id=(peer(d), col), device_id_type=MESH,
         ).wait_recv()
-    states = sbuf[...].reshape(total, cells).astype(F32)
+    states = jnp.concatenate([unpack(sbuf[z], m, pad, cells) for z in range(n)], axis=0)
     state_mean = jnp.sum(states, axis=0, keepdims=True) / members
     state_pert = jnp.where(real, states - state_mean, 0.0).astype(BF16)
 
@@ -305,7 +335,8 @@
         dests = [peer(d) for d in range(n - 1, 0, -1)]
     for d, dest in enumerate(dests + [me]):
         rows = wt[pl.ds(pl.multiple_of(dest * pad, 16), pad), :]
-        result = (state_mean + jnp.dot(rows, state_pert, preferred_element_type=F32)).astype(BF16)
+        result = (state_mean + jnp.dot(rows, state_pert, preferred_element_type=F32))
+        result = pack(result, m, oloc.shape[1:])
         if d == n - 1:
             oland[me] = result
         else:
@@ -315,7 +346,7 @@
             )
 
     def finish(source):
-        out_ref[:, pl.ds(pl.multiple_of(source * cells, 128), cells)] = oland[source, 0:m, :]
+        out_ref[:, pl.ds(pl.multiple_of(source * cells, 128), cells)] = unpack(oland[source], m, pad, cells)[0:m].astype(BF16)
 
     finish(me)
     for source in reversed(dests):
@@ -344,6 +375,7 @@
     pad = (m // 16 + 1) * 16
     total = n * pad
     block = -(-3 * (width // 128) // 8) * 8
+    obs_block, state_block = packed_shape(m, pad, width), packed_shape(m, pad, cells)
     vmem = pl.BlockSpec(memory_space=pltpu.VMEM)
     dma = pltpu.SemaphoreType.DMA
     result = pl.pallas_call(
@@ -358,9 +390,10 @@
             pltpu.VMEM((1, length), jnp.int32),
             pltpu.VMEM((1, length), F32),
             pltpu.VMEM((n, pad, cells), BF16),
-            pltpu.VMEM((n, pad, width), BF16),
-            pltpu.VMEM((n, 3, pad, width), BF16),
-            pltpu.VMEM((n, pad, cells), BF16),
+            pltpu.VMEM((n, *state_block), BF16),
+            pltpu.VMEM((n, *obs_block), BF16),
+            pltpu.VMEM((n, 3, *obs_block), BF16),
+            pltpu.VMEM((n, *state_block), BF16),
             pltpu.VMEM((3 * block, 128), F32),
             pltpu.VMEM((2, block, 128), F32),
             pltpu.VMEM((8, width), F32),
@@ -369,8 +402,8 @@
             pltpu.VMEM((2, total, total), BF16),
             pltpu.VMEM((2, total, total), BF16),
             pltpu.VMEM((total, total), BF16),
-            pltpu.VMEM((n, pad, cells), BF16),
-            pltpu.VMEM((n, pad, cells), BF16),
+            pltpu.VMEM((n, *state_block), BF16),
+            pltpu.VMEM((n, *state_block), BF16),
             dma((3 * n,)), dma((n, 3)),
             dma((n,)), dma((n,)),
             dma((2,)), dma((2,)),

time: 44.7 us -> 43.2 us (0.966)
  Pallas kernels: 43.1 us -> 41.6 us
    pallas_call x1, Pallas kernels: 43.1 us -> 41.6 us  [local(): pl.pallas_call(functools.partial(kernel, n, regs, m, pad, width, cells),...]
where the time goes in v6:
time: 43.2 us; the launch traced here: 43 us
  Pallas kernels  41.6 us (96%)
  local copies, waits for them, and re-layouts  0.8 us (2%)
  between operations  0.66 us (2%)
    pallas_call x1, Pallas kernels, local(): pl.pallas_call(functools.partial(kernel, n, regs, m, pad, width, cells),...  41.6 us

profile of v6, /device:TPU:0, one launch (start us, length us, event | category | flops | bytes accessed | tf_op | source)
XLA Modules:
  0.0 43.0 jit_solution(4933603375173048083)
XLA Ops:
  0.7 41.6 %shard_map.64 = bf16[60,4096]{1,0:T(8,128)(2,1)S(1)} custom-call(bf16[60,4096]{1,0:T(8,128)(2,1)} %bitcast.7, s32[4,512]{1,0:T(4,128)} %bitcast.8, bf16[1,512]{1,0:T(2,128)(2,1)} %bitcast.11, s32[1,2048]{1,0:T(1,128)} %bitcast.9, f32[1,2048]{1,0:T(1,128)} %bitcast.10, s32[1,1]{1,0:T(1,128)S(6)} %copy.8.count_ref), custom_call_target="tpu_custom_call" | custom-call | tf_op jit(solution)/shard_map/pallas_call | solution.py:381
  42.2 0.8 %copy.9 = bf16[60,1,4096]{2,0,1:T(8,128)(2,1)} copy(bf16[60,1,4096]{2,0,1:T(8,128)(2,1)S(1)} %bitcast.6) | data formatting | bytes 983040

commit v7 on v6

--- a/solution.py
+++ b/solution.py
@@ -123,9 +123,10 @@
     for load in loads[:3]:
         load.wait()
     tail = (m // 16) * 16
-    for q in range(n):
+
+    def fill(q):
         bgp[q, tail:pad, :] = jnp.zeros((pad - tail, cells), BF16)
-        bgp[q, 0:m, :] = bg_ref[:, q * cells:(q + 1) * cells]
+        bgp[q, 0:m, :] = bg_ref[:, pl.ds(pl.multiple_of(q * cells, 128), cells)]
 
     yloc[...] = jnp.broadcast_to(yobs_ref[...].astype(F32), yloc.shape)
     ybuf[1] = yloc[...]
@@ -138,6 +139,7 @@
     def observe(row):
         hot = lax.broadcasted_iota(jnp.int32, (cells, width), 0) == idx_ref[pl.ds(row, 1), :]
         hot = jnp.where(hot, 1.0, 0.0).astype(BF16)
+        fill(row)
         seen = jnp.dot(bgp[row], hot, preferred_element_type=F32)
         return pack(seen, m, obs_loc.shape[1:])
 

time: 43.2 us -> 43.2 us (level)
  no operation moved by 1% of the time
where the time goes in v7:
time: 43.2 us; the launch traced here: 43 us
  Pallas kernels  41.6 us (96%)
  local copies, waits for them, and re-layouts  0.8 us (2%)
  between operations  0.66 us (2%)
    pallas_call x1, Pallas kernels, local(): pl.pallas_call(functools.partial(kernel, n, regs, m, pad, width, cells),...  41.6 us

profile of v7, /device:TPU:0, one launch (start us, length us, event | category | flops | bytes accessed | tf_op | source)
XLA Modules:
  0.0 43.0 jit_solution(16474395834568029757)
XLA Ops:
  0.7 41.6 %shard_map.64 = bf16[60,4096]{1,0:T(8,128)(2,1)S(1)} custom-call(bf16[60,4096]{1,0:T(8,128)(2,1)} %bitcast.7, s32[4,512]{1,0:T(4,128)} %bitcast.8, bf16[1,512]{1,0:T(2,128)(2,1)} %bitcast.11, s32[1,2048]{1,0:T(1,128)} %bitcast.9, f32[1,2048]{1,0:T(1,128)} %bitcast.10, s32[1,1]{1,0:T(1,128)S(6)} %copy.8.count_ref), custom_call_target="tpu_custom_call" | custom-call | tf_op jit(solution)/shard_map/pallas_call | solution.py:383
  42.2 0.8 %copy.9 = bf16[60,1,4096]{2,0,1:T(8,128)(2,1)} copy(bf16[60,1,4096]{2,0,1:T(8,128)(2,1)S(1)} %bitcast.6) | data formatting | bytes 983040

commit v8 on v6

--- a/solution.py
+++ b/solution.py
@@ -246,6 +246,9 @@
                 landed(source, slot).wait_recv()
                 hand_on(i, source, slot).start()
 
+    for dest in state_later:
+        state_copies.append(state_send(dest, len(state_copies)))
+
     def take(k):
         if n != 4:
             if k == 0:
@@ -291,9 +294,6 @@
                 gacc[i] = term(values, table, slot)
             else:
                 gacc[i] += term(values, table, slot)
-        if k == 0:
-            for dest in state_later:
-                state_copies.append(state_send(dest, len(state_copies)))
     slot = take(2)
 
     values = perturbed(slot)

time: 43.2 us -> 44.2 us (1.023)
  Pallas kernels: 41.6 us -> 42.6 us
    pallas_call x1, Pallas kernels: 41.6 us -> 42.6 us  [local(): pl.pallas_call(functools.partial(kernel, n, regs, m, pad, width, cells),...]
where the time goes in v8:
time: 44.2 us; the launch traced here: 44 us
  Pallas kernels  42.6 us (96%)
  local copies, waits for them, and re-layouts  0.8 us (2%)
  between operations  0.66 us (1%)
    pallas_call x1, Pallas kernels, local(): pl.pallas_call(functools.partial(kernel, n, regs, m, pad, width, cells),...  42.6 us

profile of v8, /device:TPU:0, one launch (start us, length us, event | category | flops | bytes accessed | tf_op | source)
XLA Modules:
  0.0 44.0 jit_solution(14131401935931062521)
XLA Ops:
  0.7 42.6 %shard_map.64 = bf16[60,4096]{1,0:T(8,128)(2,1)S(1)} custom-call(bf16[60,4096]{1,0:T(8,128)(2,1)} %bitcast.7, s32[4,512]{1,0:T(4,128)} %bitcast.8, bf16[1,512]{1,0:T(2,128)(2,1)} %bitcast.11, s32[1,2048]{1,0:T(1,128)} %bitcast.9, f32[1,2048]{1,0:T(1,128)} %bitcast.10, s32[1,1]{1,0:T(1,128)S(6)} %copy.8.count_ref), custom_call_target="tpu_custom_call" | custom-call | tf_op jit(solution)/shard_map/pallas_call | solution.py:381
  43.2 0.8 %copy.9 = bf16[60,1,4096]{2,0,1:T(8,128)(2,1)} copy(bf16[60,1,4096]{2,0,1:T(8,128)(2,1)S(1)} %bitcast.6) | data formatting | bytes 983040
